TPU v7x, 128 devices: a whole 4x4x4 slice. The times are simulated.
128 devices in a mesh: tower: 2 (over y_lo), batch: 64 (over z, y_hi, x, core).
Axes of the slice: x: 4, y: 4 (y_hi: 2, y_lo: 2; y = y_hi * 2 + y_lo), z: 4, core: 2. Of those that a mesh axis runs over, the one named last changes fastest.
Arguments:
- states: bfloat16 [2, 16384, 1280], P('tower', 'batch'), may hold values from -6 to 6
- projection: bfloat16 [2, 1280, 1024], P('tower'), may hold values from -6 to 6
- prompt_ids: int32 [16384], P('batch'), may hold values from 0 to 8191
- log_temper: float32 [1], replicated, may hold values from 1.5 to 2.5
- logit_offset: float32 [1], replicated, may hold values from -6 to -2
Outputs:
- state_grad: bfloat16 [2, 16384, 1280], P('tower', 'batch')
- projection_grad: float32 [2, 1280, 1024], P('tower', 'batch')
All inputs are finite; a program needn't handle non-finite values.
Results may differ from a plain program's by a relative error of at most 0.007.
Values may be sent and summed in bfloat16 or wider, within the bound.
A program may use at most 128 MiB of HBM per device.

v0:
```python
import jax
import jax.numpy as jnp
from jax import lax
from jax.sharding import PartitionSpec as P

LOSS_SCALE = 16.0
EPSILON = 1e-06


def swapped(block, axis, apart):
    count = lax.axis_size(axis)
    route = []
    for low in range(count):
        high = low | 1 << apart
        if high != low and high < count:
            route += [(low, high), (high, low)]
    return lax.ppermute(block, axis, route)


def local(states, projection, prompt_ids, log_temper, logit_offset):
    own_states = states[0]
    weights = projection[0]
    temper = jnp.exp(log_temper[0])
    offset = logit_offset[0]
    raw_proj = jnp.dot(own_states, weights, preferred_element_type=jnp.float32)
    length_row = jnp.sqrt(jnp.sum(raw_proj * raw_proj, axis=1, keepdims=True) + EPSILON)
    unit_rows = raw_proj / length_row
    own_emb = unit_rows.astype(jnp.bfloat16)
    partner_emb = swapped(own_emb, "tower", 0)
    other_emb = lax.all_gather(partner_emb, "batch", axis=0, tiled=True)
    other_ids = lax.all_gather(prompt_ids, "batch", axis=0, tiled=True)
    logits = (
        temper
        * lax.dot_general(
            own_emb, other_emb, (((1,), (1,)), ((), ())), preferred_element_type=jnp.float32
        )
        + offset
    )
    sign_vals = jnp.where(prompt_ids[:, None] == other_ids[None, :], 1.0, -1.0).astype(jnp.float32)
    pair_grad = (-LOSS_SCALE * sign_vals * jax.nn.sigmoid(-sign_vals * logits)).astype(jnp.bfloat16)
    summed = jnp.dot(pair_grad, other_emb, preferred_element_type=jnp.float32)
    emb_grad = temper * summed
    along_unit = jnp.sum(unit_rows * emb_grad, axis=1, keepdims=True)
    raw_grad = ((emb_grad - unit_rows * along_unit) / length_row).astype(jnp.bfloat16)
    state_grad = lax.dot_general(
        raw_grad, weights, (((1,), (1,)), ((), ())), preferred_element_type=jnp.float32
    ).astype(jnp.bfloat16)
    matrix_term = lax.dot_general(
        own_states, raw_grad, (((0,), (0,)), ((), ())), preferred_element_type=jnp.float32
    )
    owned_rows = lax.psum_scatter(matrix_term, "batch", scatter_dimension=0, tiled=True)
    return (state_grad[None], owned_rows[None])


def solution(mesh):
    return jax.shard_map(
        local,
        mesh=mesh,
        in_specs=(P("tower", "batch", None), P("tower", None, None), P("batch"), P(), P()),
        out_specs=(P("tower", "batch", None), P("tower", "batch", None)),
        check_vma=False,
    )
```

profile of v0, /device:TPU:1, one launch (start us, length us, event | category | flops | bytes accessed | tf_op | source)
XLA Modules:
  0.0 886.6 jit_solution(10854627546127280555)
XLA Ops:
  7.2 0.0 copy-start
  7.2 0.0 all-gather.3.cloned.1.call-start
  7.2 1.7 copy-done
  8.9 2.0 multiply_reduce_fusion.1
  10.9 0.0 copy-start.1
  10.9 1.0 copy-done.1
  11.9 0.1 fusion.25
  12.1 0.0 copy-start.3
  12.1 0.8 copy-done.3
  12.9 2.1 collective-permute-start
  15.0 11.2 %collective-permute-done = bf16[256,1024]{1,0:T(8,128)(2,1)S(1)} collective-permute-done((bf16[256,1024]{1,0:T(8,128)(2,1)S(1)}, bf16[256,1024]{1,0:T(8,128)(2,1)S(1)}, u32[]{:S(2)}, u32[]{:S(2)}) %collective-permute-start) | collective-permute-done | bytes 524320 | tf_op jit(solution)/shard_map/ppermute | solution.py:17
  26.2 0.0 copy-start.2
  26.2 0.8 copy-done.2
  27.0 0.0 all-gather.3.cloned.1.call-update
  27.0 0.0 all-reduce.3.cloned.1.call-start
  28.4 99.0 %all-gather = s32[64,1,256]{2,1,0:T(1,128)S(1)} all-gather(s32[1,1,256]{2,1,0:T(1,128)} %bitcast.36), channel_id=1, replica_groups=mesh['tower'=2,'batch'=64] {'batch'}, dimensions={0}, use_global_device_ids=true | all-gather | bytes 66560 | tf_op jit(solution)/shard_map/all_gather | solution.py:31
  127.5 61.9 %all-gather.3.cloned.1.call-done = bf16[16384,1024]{1,0:T(8,128)(2,1)} async-done(((bf16[256,1024]{1,0:T(8,128)(2,1)}), bf16[16384,1024]{1,0:T(8,128)(2,1)}) %all-gather.3.cloned.1.call-update) | async-done | bytes 33554448 | tf_op jit(solution)/shard_map/all_gather | solution.py:30
  189.3 0.0 copy-start.4
  189.3 34.6 %multiply_reduce_fusion = (f32[256]{0:T(256)S(1)}, f32[256,1024]{1,0:T(8,128)}) fusion(f32[256,1024]{1,0:T(8,128)} %copy-done.1, f32[256]{0:T(256)S(1)} %add_sqrt_fusion, bf16[16384,1024]{1,0:T(8,128)(2,1)} %all-gather.3.cloned.1.call-done, bf16[256,1024]{1,0:T(8,128)(2,1)} %copy-done.3, f32[]{:T(128)} %bitcast.34, f32[]{:T(128)} %bitcast, ...), kind=kOutput, calls=%fused_computation.21 | convolution fusion | flops 17231249408 | bytes 36244488 | tf_op jit(solution)/shard_map/dot_general | solution.py:41
  223.9 0.0 copy-start.5
  223.9 0.0 copy-done.4
  224.0 5.0 convolution_bitcast_fusion
  229.0 0.0 all-reduce.3.cloned.1.call-update
  229.0 0.0 copy-done.5
  229.0 0.6 dynamic-slice
  230.2 3.3 fusion.16
  233.6 643.9 %all-reduce.3.cloned.1.call-done = f32[1280,1024]{0,1:T(8,128)} async-done(((f32[1280,1024]{0,1:T(8,128)}), f32[1280,1024]{0,1:T(8,128)}) %all-reduce.3.cloned.1.call-update) | async-done | bytes 5242896
  877.5 1.4 dynamic-slice_bitcast_fusion
  878.9 0.8 copy.8
  (1 shorter events, 0.0 us)
Async XLA Ops:
  7.2 1.7 copy-start
  7.2 182.1 %all-gather.3.cloned.1.call-start = ((), (), s32[]{:S(2)}) async-start(), calls=%async_computation | async-start | bytes 34078720 | tf_op jit(solution)/shard_map/all_gather | solution.py:30
  10.9 1.0 copy-start.1
  12.1 0.8 copy-start.3
  12.9 13.4 %collective-permute-start = (bf16[256,1024]{1,0:T(8,128)(2,1)S(1)}, bf16[256,1024]{1,0:T(8,128)(2,1)S(1)}, u32[]{:S(2)}, u32[]{:S(2)}) collective-permute-start(bf16[256,1024]{1,0:T(8,128)(2,1)S(1)} %fusion.25), channel_id=1, source_target_pairs={{0,64},{64,0},{1,65},{65,1},{2,66},{66,2},{3,67},{67,3},{4,68},{68... | collective-permute-start | bytes 1572872 | tf_op jit(solution)/shard_map/ppermute | solution.py:17
  26.2 0.8 copy-start.2
  27.0 850.4 %all-reduce.3.cloned.1.call-start = ((), (), s32[]{:S(2)}) async-start(), calls=%async_computation.1 | async-start | bytes 10485760
  189.3 34.6 %copy-start.4 = (bf16[1,256,1280]{2,1,0:T(8,128)(2,1)S(1)}, bf16[1,256,1280]{2,1,0:T(8,128)(2,1)}, u32[]{:S(2)}) copy-start(bf16[1,256,1280]{2,1,0:T(8,128)(2,1)} %param.5) | copy-start | bytes 1966084
  223.9 5.0 copy-start.5
Sparse Core Ops, SparseCore 0:
  27.2 162.1 all-gather.2
  229.1 648.3 all-reduce.2
where the time goes:
time: 887 us
  waiting for transfers between devices  717 us (81%)
  blocking collectives  99 us (11%)
  matrix products  45 us (5%)
  between operations  16.1 us (2%)
    unnamed x3, waiting for transfers between devices  644 us
    all_gather x1, blocking collectives, local(): other_ids = lax.all_gather(prompt_ids, 'batch', axis=0, tiled=True)  99 us
    all_gather x1, waiting for transfers between devices, local(): other_emb = lax.all_gather(partner_emb, 'batch', axis=0, tiled=True)  61.9 us
    dot_general x1, matrix products, local(): summed = jnp.dot(pair_grad, other_emb, preferred_element_type=jnp.float32)  34.6 us
  transfers between devices with their start and end apart: 3, of which 3 were waited for; matrix products, arithmetic and copies ran while one was open for 0% of the time, Pallas kernels for 0%

commit v1 on v0

v1 whole, which is shorter than its diff:
```python
import jax
import jax.numpy as jnp
from jax import lax
from jax.experimental import pallas as pl
from jax.experimental.pallas import tpu as pltpu
from jax.sharding import PartitionSpec as P

EPSILON = 1e-06
MESH = pl.DeviceIdType.MESH
F32, BF16 = jnp.float32, jnp.bfloat16
NT = (((1,), (1,)), ((), ()))
TN = (((0,), (0,)), ((), ()))
NN = (((1,), (0,)), ((), ()))

ROWS = 256
EMB = 1024
FEAT = 1280
CHUNK = 64
QS = ROWS // CHUNK
HALF = EMB // 2
FEAT_Z = FEAT // 4
OWN_ROWS = 40


class Sems:
    sizes = dict(
        y=QS, y_id=1, ring=2 * 12, ring_id=2 * 3, core=4, core_id=4, core_s=1,
        part=4, far=2 * QS, to_next=2 * QS, to_prev=2 * QS, y_back=QS,
        rg=QS, st_p=4, st_q=4, mid=2, end_p=4, end_q=4, last=1,
    )

    @classmethod
    def at(cls, name, index=0):
        base = 0
        for key, size in cls.sizes.items():
            if key == name:
                return base + index
            base += size
        raise KeyError(name)

    @classmethod
    def total(cls):
        return sum(cls.sizes.values())


def dot(a, b, dims):
    return lax.dot_general(a, b, dims, preferred_element_type=F32)


def kernel(
    s_ref, w_ref, id_ref, lt_ref, of_ref, sg_ref, pg_ref,
    blocks, ids, raw, inv, pair, grad, out_buf, far_in, near_in, part_out, part_in, y_out, y_in,
    rg, rg_mine, rg_theirs, s_other, s_t, mat, p_out, q_out, p_in, q_in, p_sum, q_sum, mid_out, mid_in,
    p_two, q_two, p_end, q_end, last_out, last_in, ssem, rsem,
):
    tower = lax.axis_index("tower")
    batch = lax.axis_index("batch")
    core = lax.rem(batch, 2)
    px = lax.rem(batch // 2, 4)
    yh = lax.rem(batch // 8, 2)
    pz = batch // 16
    other = 1 - tower

    def dev(t, z, y, x, c):
        return (t, ((z * 2 + y) * 4 + x) * 2 + c)

    def ring_x(d):
        return dev(tower, pz, yh, lax.rem(px + d, 4), core)

    def ring_z(d):
        return dev(tower, lax.rem(pz + d, 4), yh, px, core)

    def ring_of(r, d):
        return dev(tower, lax.rem(pz + r * d, 4), yh, lax.rem(px + (1 - r) * d, 4), core)

    partner = dev(tower, pz, yh, px, 1 - core)
    y_up = dev(other, pz, jnp.where(tower == 1, 1 - yh, yh), px, core)
    y_down = dev(other, pz, jnp.where(tower == 0, 1 - yh, yh), px, core)
    y_two = dev(tower, pz, 1 - yh, px, core)

    def block(r, slot):
        return slot + r * (4 + slot)

    def copy(name, index, src, dst, where):
        k = Sems.at(name) + index
        return pltpu.make_async_remote_copy(
            src_ref=src, dst_ref=dst, send_sem=ssem.at[k], recv_sem=rsem.at[k],
            device_id=where, device_id_type=MESH,
        )

    def arrived(name, index, ref):
        copy(name, index, ref, ref, partner).wait_recv()

    def left(name, index, ref):
        copy(name, index, ref, ref, partner).wait_send()

    def rows(q):
        return pl.ds(CHUNK * q, CHUNK)

    barrier = pltpu.get_barrier_semaphore()
    near = [partner, y_up, y_down, y_two] + [ring_x(d) for d in (1, 2, 3)] + [ring_z(d) for d in (1, 2, 3)]
    for where in near:
        pl.semaphore_signal(barrier, inc=1, device_id=where, device_id_type=MESH)

    @pl.loop(0, 2)
    def _(n):
        cols = pl.ds(pl.multiple_of(n * HALF, HALF), HALF)
        raw[:, cols] = dot(s_ref[...], w_ref[:, cols], NN)

    pl.semaphore_wait(barrier, len(near))

    own0 = block(tower, 0)
    oth0 = block(other, 0)

    def to_next(k, r, q):
        return copy("ring", 12 * k + q, blocks.at[block(r, 0), rows(q)], blocks.at[block(r, 1), rows(q)], ring_of(r, 1))

    def to_prev(k, r, q):
        return copy("ring", 12 * k + 4 + q, blocks.at[block(r, 0), rows(q)], blocks.at[block(r, 3), rows(q)], ring_of(r, 3))

    def onward(k, r, q):
        slot, d = (1, 1) if q < 2 else (3, 3)
        return copy("ring", 12 * k + 8 + q, blocks.at[block(r, slot), rows(q)], blocks.at[block(r, 2), rows(q)], ring_of(r, d))

    def got_next(k, r, q):
        arrived("ring", 12 * k + q, blocks.at[block(r, 1), rows(q)])

    def got_prev(k, r, q):
        arrived("ring", 12 * k + 4 + q, blocks.at[block(r, 3), rows(q)])

    def got_onward(k, r, q):
        arrived("ring", 12 * k + 8 + q, blocks.at[block(r, 2), rows(q)])

    def ids_out(k, r):
        copy("ring_id", 3 * k, ids.at[block(r, 0)], ids.at[block(r, 1)], ring_of(r, 1)).start()
        copy("ring_id", 3 * k + 1, ids.at[block(r, 0)], ids.at[block(r, 3)], ring_of(r, 3)).start()

    def ids_onward(k, r):
        arrived("ring_id", 3 * k, ids.at[block(r, 1)])
        copy("ring_id", 3 * k + 2, ids.at[block(r, 1)], ids.at[block(r, 2)], ring_of(r, 1)).start()
        arrived("ring_id", 3 * k + 1, ids.at[block(r, 3)])

    def core_send(slot):
        copy("core", slot, blocks.at[4 + 2 * slot], blocks.at[5 + 2 * slot], partner).start()
        copy("core_id", slot, ids.at[4 + 2 * slot], ids.at[5 + 2 * slot], partner).start()

    def core_got(slot):
        arrived("core", slot, blocks.at[5 + 2 * slot])
        arrived("core_id", slot, ids.at[5 + 2 * slot])

    ids[own0] = jnp.broadcast_to(id_ref[...], (8, ROWS))
    copy("y_id", 0, ids.at[own0], ids.at[own0], y_up).start()
    for q in range(QS):
        part = raw[rows(q), :]
        length = jnp.sqrt(jnp.sum(part * part, axis=1, keepdims=True) + EPSILON)
        scale = 1.0 / length
        inv[rows(q), :] = jnp.broadcast_to(scale, (CHUNK, 128))
        blocks[own0, rows(q)] = (part * scale).astype(BF16)
        copy("y", q, blocks.at[own0, rows(q)], blocks.at[own0, rows(q)], y_up).start()
        to_next(0, tower, q).start()
        if q >= 2:
            to_prev(0, tower, q).start()
    for q in range(2):
        to_prev(0, tower, q).start()
    ids_out(0, tower)

    @pl.when(tower == 1)
    def _():
        core_send(0)

    copy("core_s", 0, s_ref, s_other, partner).start()
    s_t[:, :ROWS] = s_ref[...].T

    def y_got(q):
        arrived("y", q, blocks.at[oth0, rows(q)])
        to_next(1, other, q).start()
        to_prev(1, other, q).start()

    y_got(0)
    got_next(0, tower, 0)
    onward(0, tower, 0).start()
    got_prev(0, tower, 2)
    onward(0, tower, 2).start()
    y_got(1)
    got_next(0, tower, 1)
    onward(0, tower, 1).start()
    got_prev(0, tower, 3)
    onward(0, tower, 3).start()
    ids_onward(0, tower)
    arrived("y_id", 0, ids.at[oth0])
    ids_out(1, other)
    y_got(2)
    y_got(3)

    @pl.when(tower == 0)
    def _():
        core_send(0)

    for q in range(2):
        got_next(1, other, q)
        onward(1, other, q).start()
    for q in range(2):
        got_next(0, tower, 2 + q)
        got_prev(0, tower, q)
    ids_onward(1, other)

    @pl.when(tower == 1)
    def _():
        core_send(1)
        core_send(3)
        core_got(0)
        core_got(1)
        core_got(3)

    @pl.when(tower == 0)
    def _():
        core_got(0)

    temper = jnp.exp(lt_ref[...])
    slope = 0.5 * temper
    shift = 0.5 * of_ref[...]

    def unit(a, b):
        i = jnp.where(tower == 0, a, b)
        j = jnp.where(tower == 0, b, a)
        at = pl.multiple_of(4 + 2 * j, 2)
        text = blocks[pl.ds(at, 2)].reshape(2 * ROWS, EMB)
        logit = dot(blocks[i], text, NT)
        value = jnp.tanh(logit * slope + shift) * 8.0
        row = jnp.concatenate([ids[at, 0:1, :], ids[at + 1, 0:1, :]], axis=1).astype(F32)
        col = jnp.broadcast_to(ids[i, 0:1, :].astype(F32), (128, ROWS)).T
        same = jnp.concatenate([col] * 4, axis=1) == row
        value = value + jnp.where(same, -8.0, 8.0)
        here = pl.ds(pl.multiple_of(i * ROWS, ROWS), ROWS)
        pair[here, pl.ds(pl.multiple_of(j * 2 * ROWS, 2 * ROWS), 2 * ROWS)] = value.astype(BF16)

    @pl.loop(0, 3)
    def _(u):
        unit(u + u // 2, 0)

    for q in (2, 3):
        got_prev(1, other, q)
        onward(1, other, q).start()
    for q in (0, 1):
        got_prev(1, other, q)
        got_next(1, other, q + 2)

    @pl.when(tower == 0)
    def _():
        core_send(1)
        core_send(3)

    for q in range(QS):
        got_onward(0, tower, q)
    arrived("ring_id", 2, ids.at[block(tower, 2)])

    @pl.when(tower == 1)
    def _():
        core_send(2)

    @pl.when(tower == 0)
    def _():
        core_got(1)
        core_got(3)

    @pl.loop(0, 6)
    def _(u):
        a = u // 2
        unit(a + a // 2, 1 + 2 * lax.rem(u, 2))

    @pl.when(tower == 1)
    def _():
        core_got(2)

    @pl.loop(0, 3)
    def _(u):
        unit(2, u + u // 2)

    arrived("core_s", 0, s_other)
    s_t[:, ROWS:] = s_other[...].T

    for q in range(QS):
        got_onward(1, other, q)
    arrived("ring_id", 5, ids.at[block(other, 2)])

    @pl.when(tower == 0)
    def _():
        core_send(2)
        core_got(2)

    @pl.loop(0, 4)
    def _(u):
        unit(u, 2)

    def text_terms(half, slot):
        audio = blocks[pl.ds(0, 4)].reshape(4 * ROWS, EMB)
        return dot(pair[:, pl.ds((2 * slot + half) * ROWS, ROWS)], audio, TN)

    def audio_terms(slot):
        @pl.loop(0, 2)
        def _(n):
            cols = pl.ds(pl.multiple_of(n * HALF, HALF), HALF)
            text = blocks[pl.ds(4, 8), :, cols].reshape(8 * ROWS, HALF)
            grad[0, slot, :, cols] = dot(pair[pl.ds(slot * ROWS, ROWS), :], text, NN)

    def give(slot):
        part_out[slot] = text_terms(1, slot).astype(BF16)
        copy("part", slot, part_out.at[slot], part_in.at[slot], partner).start()

    def keep(slot):
        grad[1, slot] = text_terms(0, slot)
        arrived("part", slot, part_in.at[slot])
        grad[1, slot] += part_in[slot].astype(F32)

    def far_copy(r, q):
        return copy("far", QS * r + q, out_buf.at[r, 2, rows(q)], far_in.at[r, rows(q)], ring_of(r, 1 if q < 2 else 3))

    def next_copy(r, q):
        return copy("to_next", QS * r + q, out_buf.at[r, 3, rows(q)], near_in.at[r, 0, rows(q)], ring_of(r, 1))

    def prev_copy(r, q):
        return copy("to_prev", QS * r + q, out_buf.at[r, 1, rows(q)], near_in.at[r, 1, rows(q)], ring_of(r, 3))

    def send_far(r):
        out_buf[r, 2] = grad[r, 2].astype(BF16)
        for q in (0, 2, 1, 3):
            far_copy(r, q).start()

    def send_next(r):
        for q in range(QS):
            term = grad[r, 3, rows(q), :]
            if q < 2:
                arrived("far", QS * r + q, far_in.at[r, rows(q)])
                term += far_in[r, rows(q), :].astype(F32)
            out_buf[r, 3, rows(q), :] = term.astype(BF16)
            next_copy(r, q).start()

    def send_prev(r):
        for q in range(QS):
            term = grad[r, 1, rows(q), :]
            if q >= 2:
                arrived("far", QS * r + q, far_in.at[r, rows(q)])
                term += far_in[r, rows(q), :].astype(F32)
            out_buf[r, 1, rows(q), :] = term.astype(BF16)
            prev_copy(r, q).start()

    give(2)
    audio_terms(2)
    send_far(0)
    keep(2)
    send_far(1)
    give(3)
    give(1)
    audio_terms(3)
    send_next(0)
    audio_terms(1)
    send_prev(0)
    keep(3)
    send_next(1)
    keep(1)
    send_prev(1)
    give(0)
    audio_terms(0)
    keep(0)

    def reduced(r, q):
        arrived("to_next", QS * r + q, near_in.at[r, 0, rows(q)])
        arrived("to_prev", QS * r + q, near_in.at[r, 1, rows(q)])
        return (
            grad[r, 0, rows(q), :]
            + near_in[r, 0, rows(q), :].astype(F32)
            + near_in[r, 1, rows(q), :].astype(F32)
        )

    def back_copy(q):
        return copy("y_back", q, y_out.at[rows(q)], y_in.at[rows(q)], y_down)

    for q in range(QS):
        y_out[rows(q), :] = reduced(other, q).astype(BF16)
        back_copy(q).start()

    def rg_copy(q):
        return copy("rg", q, rg_theirs.at[rows(q)], rg_mine.at[pl.ds(ROWS + CHUNK * q, CHUNK)], partner)

    for q in range(QS):
        total = reduced(tower, q)
        arrived("y_back", q, y_in.at[rows(q)])
        emb_grad = temper * (total + y_in[rows(q), :].astype(F32))
        scale = inv[rows(q), 0:1]
        unit_rows = raw[rows(q), :] * scale
        along = jnp.sum(unit_rows * emb_grad, axis=1, keepdims=True)
        value = ((emb_grad - unit_rows * along) * scale).astype(BF16)
        rg[rows(q), :] = value
        low, high = value[:, :HALF], value[:, HALF:]
        rg_mine[rows(q), :] = jnp.where(core == 0, low, high)
        rg_theirs[rows(q), :] = jnp.where(core == 0, high, low)
        rg_copy(q).start()

    for q in range(QS):
        arrived("rg", q, rg_mine.at[pl.ds(ROWS + CHUNK * q, CHUNK)])

    @pl.loop(0, FEAT // 256)
    def _(n):
        here = pl.ds(pl.multiple_of(n * 256, 256), 256)
        mat[here, :] = dot(s_t[here, :], rg_mine[...], NN)

    def z_rows(d):
        at = pl.ds(pl.multiple_of(lax.rem(pz + d, 4) * FEAT_Z, FEAT_Z), FEAT_Z)
        return mat[at, :256]

    def x_rows(d):
        pieces = []
        for k in range(8):
            at = pl.multiple_of(k * 4 * OWN_ROWS + lax.rem(px + d, 4) * OWN_ROWS, 8)
            pieces.append(mat[pl.ds(at, OWN_ROWS), 256:])
        return jnp.concatenate(pieces, axis=0)

    def p_copy(d):
        return copy("st_p", d, p_out.at[d], p_in.at[d], ring_z(d))

    def q_copy(d):
        return copy("st_q", d, q_out.at[d], q_in.at[d], ring_x(d))

    for d in (2, 1, 3):
        p_out[d] = z_rows(d).astype(BF16)
        p_copy(d).start()
        q_out[d] = x_rows(d).astype(BF16)
        q_copy(d).start()

    @pl.loop(0, FEAT // 256)
    def _(n):
        here = pl.ds(pl.multiple_of(n * 256, 256), 256)
        sg_ref[:, here] = dot(rg[...], w_ref[here, :], NT).astype(BF16)

    p_one = z_rows(0)
    for d in (1, 3, 2):
        arrived("st_p", d, p_in.at[d])
        p_one += p_in[d].astype(F32)
    p_sum[...] = p_one
    at = pl.multiple_of((1 - yh) * 4 * OWN_ROWS, 8)
    mid_out[0] = p_sum[pl.ds(at, 4 * OWN_ROWS), :].astype(BF16)
    copy("mid", 0, mid_out.at[0], mid_in.at[0], y_two).start()

    def q_rows(y):
        pieces = []
        for k in range(4):
            at = pl.multiple_of(k * 2 * OWN_ROWS + y * OWN_ROWS, 8)
            pieces.append(q_sum[pl.ds(at, OWN_ROWS), :])
        return jnp.concatenate(pieces, axis=0)

    q_one = x_rows(0)
    for d in (1, 3, 2):
        arrived("st_q", d, q_in.at[d])
        q_one += q_in[d].astype(F32)
    q_sum[...] = q_one
    mid_out[1] = q_rows(1 - yh).astype(BF16)
    copy("mid", 1, mid_out.at[1], mid_in.at[1], y_two).start()

    arrived("mid", 0, mid_in.at[0])
    at = pl.multiple_of(yh * 4 * OWN_ROWS, 8)
    p_two[...] = p_sum[pl.ds(at, 4 * OWN_ROWS), :] + mid_in[0].astype(F32)

    def end_rows(p, d):
        return pl.ds(pl.multiple_of(lax.rem(p + d, 4) * OWN_ROWS, 8), OWN_ROWS)

    def p_last(d):
        return copy("end_p", d, p_two.at[end_rows(px, d)], p_end.at[d], ring_x(d))

    def q_last(d):
        return copy("end_q", d, q_two.at[end_rows(pz, d)], q_end.at[d], ring_z(d))

    for d in (2, 1, 3):
        p_last(d).start()
    arrived("mid", 1, mid_in.at[1])
    q_two[...] = q_rows(yh) + mid_in[1].astype(F32)
    for d in (2, 1, 3):
        q_last(d).start()

    p_fin = p_two[end_rows(px, 0), :]
    q_fin = q_two[end_rows(pz, 0), :]
    for d in (1, 3, 2):
        arrived("end_p", d, p_end.at[d])
        p_fin += p_end[d]
    for d in (1, 3, 2):
        arrived("end_q", d, q_end.at[d])
        q_fin += q_end[d]
    both = jnp.concatenate([p_fin, q_fin], axis=1)
    first, second = both[:20], both[20:]
    theirs = jnp.where(core == 0, second, first)
    mine = jnp.where(core == 0, first, second)
    last_out[...] = jnp.concatenate([theirs, jnp.zeros((4, HALF), F32)], axis=0)
    copy("last", 0, last_out, last_in, partner).start()
    arrived("last", 0, last_in)
    got = last_in[:20, :]
    pg_ref[:, :HALF] = jnp.where(core == 0, mine, got)
    pg_ref[:, HALF:] = jnp.where(core == 0, got, mine)

    some = blocks.at[0]
    for q in range(QS):
        left("y", q, some.at[rows(q)])
        left("y_back", q, some.at[rows(q)])
        left("rg", q, rg_theirs.at[rows(q)])
    left("y_id", 0, ids.at[0])
    for k in range(24):
        left("ring", k, some.at[rows(0)])
    for k in range(6):
        left("ring_id", k, ids.at[0])
    for k in range(4):
        left("core", k, some)
        left("core_id", k, ids.at[0])
        left("part", k, some)
    left("core_s", 0, s_other)
    for k in range(2 * QS):
        left("far", k, some.at[rows(0)])
        left("to_next", k, some.at[rows(0)])
        left("to_prev", k, some.at[rows(0)])
    for d in (1, 2, 3):
        left("st_p", d, p_out.at[d])
        left("st_q", d, q_out.at[d])
        left("end_p", d, p_end.at[d])
        left("end_q", d, q_end.at[d])
    for k in range(2):
        left("mid", k, mid_out.at[k])
    left("last", 0, last_out)


def local(states, projection, prompt_ids, log_temper, logit_offset):
    vmem = pl.BlockSpec(memory_space=pltpu.VMEM)
    scratch = [
        ((12, ROWS, EMB), BF16),
        ((12, 8, ROWS), jnp.int32),
        ((ROWS, EMB), F32),
        ((ROWS, 128), F32),
        ((4 * ROWS, 8 * ROWS), BF16),
        ((2, 4, ROWS, EMB), F32),
        ((2, 4, ROWS, EMB), BF16),
        ((2, ROWS, EMB), BF16),
        ((2, 2, ROWS, EMB), BF16),
        ((4, ROWS, EMB), BF16),
        ((4, ROWS, EMB), BF16),
        ((ROWS, EMB), BF16),
        ((ROWS, EMB), BF16),
        ((ROWS, EMB), BF16),
        ((2 * ROWS, HALF), BF16),
        ((ROWS, HALF), BF16),
        ((ROWS, FEAT), BF16),
        ((FEAT, 2 * ROWS), BF16),
        ((FEAT, HALF), F32),
        ((4, FEAT_Z, 256), BF16),
        ((4, FEAT_Z, 256), BF16),
        ((4, FEAT_Z, 256), BF16),
        ((4, FEAT_Z, 256), BF16),
        ((FEAT_Z, 256), F32),
        ((FEAT_Z, 256), F32),
        ((2, FEAT_Z // 2, 256), BF16),
        ((2, FEAT_Z // 2, 256), BF16),
        ((FEAT_Z // 2, 256), F32),
        ((FEAT_Z // 2, 256), F32),
        ((4, OWN_ROWS, 256), F32),
        ((4, OWN_ROWS, 256), F32),
        ((24, HALF), F32),
        ((24, HALF), F32),
    ]
    state_grad, owned = pl.pallas_call(
        kernel,
        out_shape=(
            jax.ShapeDtypeStruct((ROWS, FEAT), BF16),
            jax.ShapeDtypeStruct((20, EMB), F32),
        ),
        in_specs=[vmem] * 5,
        out_specs=(vmem, vmem),
        scratch_shapes=[pltpu.VMEM(shape, kind) for shape, kind in scratch]
        + [pltpu.SemaphoreType.DMA((Sems.total(),)), pltpu.SemaphoreType.DMA((Sems.total(),))],
        compiler_params=pltpu.CompilerParams(
            collective_id=0, has_side_effects=True, vmem_limit_bytes=60 * 2**20
        ),
        name="contrast",
    )(
        states[0],
        projection[0],
        prompt_ids.reshape(1, ROWS),
        log_temper.reshape(1, 1),
        logit_offset.reshape(1, 1),
    )
    return state_grad[None], owned[None]


def solution(mesh):
    return jax.shard_map(
        local,
        mesh=mesh,
        in_specs=(P("tower", "batch", None), P("tower", None, None), P("batch"), P(), P()),
        out_specs=(P("tower", "batch", None), P("tower", "batch", None)),
        check_vma=False,
    )
```

time: 887 us -> 103 us (0.12)
  waiting for transfers between devices: 717 us -> 0 us
  blocking collectives: 99 us -> 0 us
  Pallas kernels: 0 us -> 96.4 us
  matrix products: 45 us -> 0 us
  between operations: 16.1 us -> 1.93 us
    unnamed x3 -> x0, waiting for transfers between devices: 644 us -> none
    all_gather x1 -> x0, blocking collectives: 99 us -> none  [local(): other_ids = lax.all_gather(prompt_ids, 'batch', axis=0, tiled=True)]
    pallas_call x0 -> x1, Pallas kernels: none -> 96.4 us  [local(): pl.pallas_call(kernel, out_shape=(jax.ShapeDtypeStruct((ROWS, FEAT), BF16...]
    all_gather x1 -> x0, waiting for transfers between devices: 61.9 us -> none  [local(): other_emb = lax.all_gather(partner_emb, 'batch', axis=0, tiled=True)]
    dot_general x4 -> x0, matrix products: 45 us -> none  [the longest x1 34.6 us: local(): summed = jnp.dot(pair_grad, other_emb, preferred_element_type=jnp.float32)]
    ppermute x1 -> x0, waiting for transfers between devices: 11.2 us -> none  [swapped(): return lax.ppermute(block, axis, route)]
  transfers between devices with their start and end apart: 3 -> 0, of which waited for: 3 -> 0; matrix products, arithmetic and copies ran while one was open for 0% -> 0% of each run, Pallas kernels for 0% -> 0%
where the time goes in v1:
time: 103 us; the launch traced here: 102 us
  Pallas kernels  96.4 us (94%)
  local copies, waits for them, and re-layouts  3.58 us (3%)
  between operations  1.93 us (2%)
    pallas_call x1, Pallas kernels, local(): pl.pallas_call(kernel, out_shape=(jax.ShapeDtypeStruct((ROWS, FEAT), BF16...  96.4 us
    unnamed x2, local copies, waits for them, and re-layouts  3.58 us

profile of v1, /device:TPU:1, one launch (start us, length us, event | category | flops | bytes accessed | tf_op | source)
XLA Modules:
  0.0 101.9 jit_solution(6220297938363712993)
XLA Ops:
  1.9 96.4 %contrast.1 = (bf16[256,1280]{1,0:T(8,128)(2,1)}, f32[20,1024]{1,0:T(8,128)}) custom-call(bf16[256,1280]{1,0:T(8,128)(2,1)} %bitcast.11, bf16[1280,1024]{1,0:T(8,128)(2,1)} %bitcast.9, s32[1,256]{1,0:T(1,128)} %bitcast.13, f32[1,1]{1,0:T(1,128)} %bitcast.7.lt_ref, f32[1,1]{1,0:T(1,128)} %bitcast.8.of_ref), custom_call_target="tpu_custom_call" | custom-call | tf_op jit(solution)/shard_map/contrast/pallas_call | solution.py:564
  98.3 1.6 %copy.7 = f32[1,20,1024]{2,0,1:T(1,128)} copy(f32[1,20,1024]{2,1,0:T(8,128)} %bitcast.12) | data formatting | bytes 163840
  99.9 2.0 %copy.11 = bf16[1,256,1280]{2,1,0:T(8,128)(2,1)} copy(bf16[1,256,1280]{2,1,0:T(8,128)(2,1)} %bitcast.10) | data formatting | bytes 1310720

commit v2 on v1

v2 whole, which is shorter than its diff:
```python
import jax
import jax.numpy as jnp
from jax import lax
from jax.experimental import pallas as pl
from jax.experimental.pallas import tpu as pltpu
from jax.sharding import PartitionSpec as P

EPSILON = 1e-06
MESH = pl.DeviceIdType.MESH
F32, BF16 = jnp.float32, jnp.bfloat16
NT = (((1,), (1,)), ((), ()))
TN = (((0,), (0,)), ((), ()))
NN = (((1,), (0,)), ((), ()))

ROWS = 256
EMB = 1024
FEAT = 1280
CHUNK = 32
QS = ROWS // CHUNK
HALF = EMB // 2
FEAT_Z = FEAT // 4
OWN_ROWS = 40
OTHER0 = 8

Y_ORDER = (0, 4, 1, 5, 2, 6, 3, 7)
NEXT_ORDER = (0, 1, 2, 3, 6, 7, 4, 5)
PREV_ORDER = (4, 5, 6, 7, 0, 1, 2, 3)
BACK_NEXT = (4, 5, 0, 1, 2, 3, 6, 7)
BACK_PREV = ((2, 3, 4, 5, 6, 7, 0, 1), (4, 5, 6, 7, 2, 3))
BACK_ORDER = (4, 5, 6, 0, 7, 1, 2, 3)


class Sems:
    sizes = dict(
        y=QS, y_id=1, ring=2 * 3 * QS, ring_id=2 * 3, core=4, core_id=4, core_s=1, extra=4,
        part=4, far=2 * QS, to_next=2 * QS, to_prev=2 * QS, y_extra=4, y_back=QS,
        rg=QS, st_p=4, st_q=4, mid=2, end_p=4, end_q=4, last=1,
    )

    @classmethod
    def at(cls, name, index=0):
        base = 0
        for key, size in cls.sizes.items():
            if key == name:
                return base + index
            base += size
        raise KeyError(name)

    @classmethod
    def total(cls):
        return sum(cls.sizes.values())


def dot(a, b, dims):
    return lax.dot_general(a, b, dims, preferred_element_type=F32)


def kernel(
    s_hbm, w_hbm, id_ref, lt_ref, of_ref, sg_ref, pg_ref,
    s_ref, w_ref, blocks, ids, raw, inv, pair, grad, out_buf, far_in, near_in, extra_out, extra_in, part_out, part_in, y_out, y_in,
    rg, rg_mine, rg_theirs, s_other, s_t, mat, p_out, q_out, p_in, q_in, p_sum, q_sum, mid_out, mid_in,
    p_two, q_two, p_end, q_end, last_out, last_in, lsem, ssem, rsem,
):
    tower = lax.axis_index("tower")
    batch = lax.axis_index("batch")
    core = lax.rem(batch, 2)
    px = lax.rem(batch // 2, 4)
    yh = lax.rem(batch // 8, 2)
    pz = batch // 16
    other = 1 - tower

    def dev(t, z, y, x, c):
        return (t, ((z * 2 + y) * 4 + x) * 2 + c)

    def ring_x(d):
        return dev(tower, pz, yh, lax.rem(px + d, 4), core)

    def ring_z(d):
        return dev(tower, lax.rem(pz + d, 4), yh, px, core)

    def ring(k, d):
        r = tower if k == 0 else other
        return dev(tower, lax.rem(pz + r * d, 4), yh, lax.rem(px + (1 - r) * d, 4), core)

    partner = dev(tower, pz, yh, px, 1 - core)
    y_up = dev(other, pz, jnp.where(tower == 1, 1 - yh, yh), px, core)
    y_down = dev(other, pz, jnp.where(tower == 0, 1 - yh, yh), px, core)
    y_two = dev(tower, pz, 1 - yh, px, core)

    def block(k, slot):
        return 2 * slot if k == 0 else OTHER0 + slot

    def copy(name, index, src, dst, where):
        n = Sems.at(name) + index
        return pltpu.make_async_remote_copy(
            src_ref=src, dst_ref=dst, send_sem=ssem.at[n], recv_sem=rsem.at[n],
            device_id=where, device_id_type=MESH,
        )

    def arrived(name, index, ref):
        copy(name, index, ref, ref, partner).wait_recv()

    def left(name, index, ref):
        copy(name, index, ref, ref, partner).wait_send()

    def rows(q):
        return pl.ds(CHUNK * q, CHUNK)

    def piece(k, slot, q):
        return blocks.at[block(k, slot), rows(q)]

    barrier = pltpu.get_barrier_semaphore()
    near = [partner, y_up, y_down, y_two] + [ring_x(d) for d in (1, 2, 3)] + [ring_z(d) for d in (1, 2, 3)]
    for where in near:
        pl.semaphore_signal(barrier, inc=1, device_id=where, device_id_type=MESH)

    def halves(n):
        return pl.ds(n * HALF, HALF)

    loads = [pltpu.make_async_copy(s_hbm, s_ref, lsem.at[0])]
    loads += [pltpu.make_async_copy(w_hbm.at[:, halves(n)], w_ref.at[:, halves(n)], lsem.at[1 + n]) for n in range(2)]
    for load in loads:
        load.start()
    ids[0] = jnp.broadcast_to(id_ref[...], (8, ROWS))
    loads[0].wait()
    for n in range(2):
        loads[1 + n].wait()
        raw[:, halves(n)] = dot(s_ref[...], w_ref[:, halves(n)], NN)

    pl.semaphore_wait(barrier, len(near))

    def to_next(k, q):
        return copy("ring", 3 * QS * k + q, piece(k, 0, q), piece(k, 1, q), ring(k, 1))

    def to_prev(k, q):
        return copy("ring", 3 * QS * k + QS + q, piece(k, 0, q), piece(k, 3, q), ring(k, 3))

    def onward(k, q):
        slot = 1 if q < QS // 2 else 3
        return copy("ring", 3 * QS * k + 2 * QS + q, piece(k, slot, q), piece(k, 2, q), ring(k, slot))

    def got_next(k, q):
        arrived("ring", 3 * QS * k + q, piece(k, 1, q))

    def got_prev(k, q):
        arrived("ring", 3 * QS * k + QS + q, piece(k, 3, q))

    def got_onward(k, q):
        arrived("ring", 3 * QS * k + 2 * QS + q, piece(k, 2, q))

    def extra(n):
        slot, q = ((1, 6), (1, 7), (3, 0), (3, 1))[n]
        return copy("extra", n, piece(0, slot, q), piece(1, slot, q), y_up)

    def got_extra(n):
        slot, q = ((1, 6), (1, 7), (3, 0), (3, 1))[n]
        arrived("extra", n, piece(1, slot, q))

    def ids_out(k):
        copy("ring_id", 3 * k, ids.at[block(k, 0)], ids.at[block(k, 1)], ring(k, 1)).start()
        copy("ring_id", 3 * k + 1, ids.at[block(k, 0)], ids.at[block(k, 3)], ring(k, 3)).start()

    def ids_onward(k):
        arrived("ring_id", 3 * k, ids.at[block(k, 1)])
        copy("ring_id", 3 * k + 2, ids.at[block(k, 1)], ids.at[block(k, 2)], ring(k, 1)).start()
        arrived("ring_id", 3 * k + 1, ids.at[block(k, 3)])

    def core_send(slot):
        copy("core", slot, blocks.at[2 * slot], blocks.at[2 * slot + 1], partner).start()
        copy("core_id", slot, ids.at[2 * slot], ids.at[2 * slot + 1], partner).start()

    def core_got(slot):
        arrived("core", slot, blocks.at[2 * slot + 1])
        arrived("core_id", slot, ids.at[2 * slot + 1])

    copy("y_id", 0, ids.at[0], ids.at[OTHER0], y_up).start()
    ids_out(0)
    for m, q in enumerate(Y_ORDER):
        part = raw[rows(q), :]
        length = jnp.sqrt(jnp.sum(part * part, axis=1, keepdims=True) + EPSILON)
        scale = 1.0 / length
        inv[rows(q), :] = jnp.broadcast_to(scale, (CHUNK, 128))
        blocks[0, rows(q)] = (part * scale).astype(BF16)
        copy("y", q, piece(0, 0, q), piece(1, 0, q), y_up).start()
        if m < 6:
            (to_next(0, q) if q < 4 else to_prev(0, q)).start()
    for q in (3, 6, 7, 4, 5):
        to_next(0, q).start()
    for q in (7, 0, 1, 2, 3):
        to_prev(0, q).start()
    core_send(0)
    copy("core_s", 0, s_ref, s_other, partner).start()
    s_t[:, :ROWS] = s_ref[...].T

    def step(m):
        q = Y_ORDER[m]
        arrived("y", q, piece(1, 0, q))
        if q < 6:
            to_next(1, q).start()
        if q >= 2:
            to_prev(1, q).start()
        q = NEXT_ORDER[m]
        got_next(0, q)
        if q < 4:
            onward(0, q).start()
        elif q >= 6:
            extra(q - 6).start()
        q = PREV_ORDER[m]
        got_prev(0, q)
        if q >= 4:
            onward(0, q).start()
        elif q < 2:
            extra(2 + q).start()

    def pass_next(q):
        got_next(1, q)
        onward(1, q).start()

    def pass_prev(q):
        got_prev(1, q)
        onward(1, q).start()

    step(0)
    step(1)
    ids_onward(0)
    arrived("y_id", 0, ids.at[OTHER0])
    ids_out(1)
    arrived("core_s", 0, s_other)
    s_t[:, ROWS:] = s_other[...].T
    step(2)
    step(3)
    pass_next(0)
    step(4)
    pass_prev(4)
    step(5)
    pass_next(1)
    step(6)
    pass_prev(5)
    step(7)
    core_send(1)
    core_send(3)
    ids_onward(1)
    pass_next(2)
    core_got(0)
    core_got(1)
    core_got(3)

    temper = jnp.exp(jnp.full((1, 1), lt_ref[0], F32))
    slope = 0.5 * temper
    shift = jnp.full((1, 1), 0.5 * of_ref[0], F32)

    def unit(a, b):
        at = pl.multiple_of(2 * b, 2)
        own = blocks[pl.ds(at, 2)].reshape(2 * ROWS, EMB)
        logit = dot(blocks[OTHER0 + a], own, NT)
        value = jnp.tanh(logit * slope + shift) * 8.0
        row = jnp.concatenate([ids[at, 0:1, :], ids[at + 1, 0:1, :]], axis=1).astype(F32)
        col = jnp.broadcast_to(ids[OTHER0 + a, 0:1, :].astype(F32), (128, ROWS)).T
        same = jnp.concatenate([col] * 4, axis=1) == row
        value = value + jnp.where(same, -8.0, 8.0)
        here = pl.ds(pl.multiple_of(a * ROWS, ROWS), ROWS)
        pair[here, pl.ds(pl.multiple_of(b * 2 * ROWS, 2 * ROWS), 2 * ROWS)] = value.astype(BF16)

    @pl.loop(0, 3)
    def _(u):
        unit(0, u + u // 2)

        @pl.when(u == 0)
        def _():
            pass_prev(6)

        @pl.when(u == 1)
        def _():
            pass_next(3)

        @pl.when(u == 2)
        def _():
            pass_prev(7)

    for q in (4, 5):
        got_next(1, q)
    for q in (2, 3):
        got_prev(1, q)
    for n in range(4):
        got_extra(n)
    for q in range(QS):
        got_onward(0, q)
    arrived("ring_id", 2, ids.at[block(0, 2)])
    core_send(2)

    @pl.loop(0, 6)
    def _(u):
        a = u // 3
        b = u - 3 * a
        unit(1 + 2 * a, b + b // 2)

    core_got(2)
    for q in range(QS):
        got_onward(1, q)
    arrived("ring_id", 5, ids.at[block(1, 2)])

    @pl.loop(0, 4)
    def _(u):
        unit(2, u)

    def own_terms(half, slot):
        rest = blocks[pl.ds(OTHER0, 4)].reshape(4 * ROWS, EMB)
        return dot(pair[:, pl.ds((2 * slot + half) * ROWS, ROWS)], rest, TN)

    def other_terms(slot):
        @pl.loop(0, 2)
        def _(n):
            cols = pl.ds(pl.multiple_of(n * HALF, HALF), HALF)
            own = blocks[pl.ds(0, 8), :, cols].reshape(8 * ROWS, HALF)
            grad[1, slot, :, cols] = dot(pair[pl.ds(slot * ROWS, ROWS), :], own, NN)

    def give(slot):
        part_out[slot] = own_terms(1, slot).astype(BF16)
        copy("part", slot, part_out.at[slot], part_in.at[slot], partner).start()

    def keep(slot):
        grad[0, slot] = own_terms(0, slot)
        arrived("part", slot, part_in.at[slot])
        grad[0, slot] += part_in[slot].astype(F32)

    def far_copy(k, q):
        return copy("far", QS * k + q, out_buf.at[k, 2, rows(q)], far_in.at[k, rows(q)], ring(k, 1 if q < 4 else 3))

    def next_copy(k, q):
        return copy("to_next", QS * k + q, out_buf.at[k, 3, rows(q)], near_in.at[k, 0, rows(q)], ring(k, 1))

    def prev_copy(k, q):
        return copy("to_prev", QS * k + q, out_buf.at[k, 1, rows(q)], near_in.at[k, 1, rows(q)], ring(k, 3))

    def extra_of(slot, q):
        if (slot, q) in ((3, 6), (3, 7), (1, 0), (1, 1)):
            return {(3, 6): 0, (3, 7): 1, (1, 0): 2, (1, 1): 3}[slot, q]
        return None

    def extra_back(n):
        return copy("y_extra", n, extra_out.at[rows(n)], extra_in.at[rows(n)], y_down)

    def send_far(k):
        for q in (0, 4, 1, 5, 2, 6, 3, 7):
            out_buf[k, 2, rows(q), :] = grad[k, 2, rows(q), :].astype(BF16)
            far_copy(k, q).start()

    def send_extra(slot):
        for q in range(QS):
            n = extra_of(slot, q)
            if n is not None:
                extra_out[rows(n), :] = grad[1, slot, rows(q), :].astype(BF16)
                extra_back(n).start()

    def send_near(k, slot, order, make):
        for q in order:
            n = extra_of(slot, q)
            if n is not None and k == 1:
                continue
            term = grad[k, slot, rows(q), :]
            if (q < 4) == (slot == 3):
                arrived("far", QS * k + q, far_in.at[k, rows(q)])
                term += far_in[k, rows(q), :].astype(F32)
            if n is not None:
                arrived("y_extra", n, extra_in.at[rows(n)])
                term += extra_in[rows(n), :].astype(F32)
            out_buf[k, slot, rows(q), :] = term.astype(BF16)
            make(k, q).start()

    other_terms(2)
    send_far(1)

    @pl.loop(0, 3)
    def _(u):
        unit(u + u // 2, 2)

    give(2)
    other_terms(3)
    send_extra(3)
    send_near(1, 3, BACK_NEXT, next_copy)
    keep(2)
    send_far(0)
    other_terms(1)
    send_extra(1)
    send_near(1, 1, BACK_PREV[1], prev_copy)
    give(3)
    give(1)
    keep(3)
    send_near(0, 3, BACK_NEXT, next_copy)
    keep(1)
    send_near(0, 1, BACK_PREV[0], prev_copy)
    other_terms(0)
    give(0)
    keep(0)

    def reduced(k, q):
        total = grad[k, 0, rows(q), :]
        if k == 0 or extra_of(3, q) is None:
            arrived("to_next", QS * k + q, near_in.at[k, 0, rows(q)])
            total += near_in[k, 0, rows(q), :].astype(F32)
        if k == 0 or extra_of(1, q) is None:
            arrived("to_prev", QS * k + q, near_in.at[k, 1, rows(q)])
            total += near_in[k, 1, rows(q), :].astype(F32)
        return total

    def back_copy(q):
        return copy("y_back", q, y_out.at[rows(q)], y_in.at[rows(q)], y_down)

    for q in BACK_ORDER:
        y_out[rows(q), :] = reduced(1, q).astype(BF16)
        back_copy(q).start()

    def rg_copy(q):
        return copy("rg", q, rg_theirs.at[rows(q)], rg_mine.at[pl.ds(ROWS + CHUNK * q, CHUNK)], partner)

    for q in BACK_ORDER:
        total = reduced(0, q)
        arrived("y_back", q, y_in.at[rows(q)])
        emb_grad = temper * (total + y_in[rows(q), :].astype(F32))
        scale = inv[rows(q), 0:1]
        unit_rows = raw[rows(q), :] * scale
        along = jnp.sum(unit_rows * emb_grad, axis=1, keepdims=True)
        value = ((emb_grad - unit_rows * along) * scale).astype(BF16)
        rg[rows(q), :] = value
        low, high = value[:, :HALF], value[:, HALF:]
        rg_mine[rows(q), :] = jnp.where(core == 0, low, high)
        rg_theirs[rows(q), :] = jnp.where(core == 0, high, low)
        rg_copy(q).start()

    for q in range(QS):
        arrived("rg", q, rg_mine.at[pl.ds(ROWS + CHUNK * q, CHUNK)])

    @pl.loop(0, FEAT // 256)
    def _(n):
        here = pl.ds(pl.multiple_of(n * 256, 256), 256)
        mat[here, :] = dot(s_t[here, :], rg_mine[...], NN)

    def z_rows(d):
        at = pl.ds(pl.multiple_of(lax.rem(pz + d, 4) * FEAT_Z, FEAT_Z), FEAT_Z)
        return mat[at, :256]

    def x_rows(d):
        pieces = []
        for k in range(8):
            at = pl.multiple_of(k * 4 * OWN_ROWS + lax.rem(px + d, 4) * OWN_ROWS, 8)
            pieces.append(mat[pl.ds(at, OWN_ROWS), 256:])
        return jnp.concatenate(pieces, axis=0)

    def p_copy(d):
        return copy("st_p", d, p_out.at[d], p_in.at[d], ring_z(d))

    def q_copy(d):
        return copy("st_q", d, q_out.at[d], q_in.at[d], ring_x(d))

    for d in (2, 1, 3):
        p_out[d] = z_rows(d).astype(BF16)
        p_copy(d).start()
        q_out[d] = x_rows(d).astype(BF16)
        q_copy(d).start()

    @pl.loop(0, FEAT // 256)
    def _(n):
        here = pl.ds(pl.multiple_of(n * 256, 256), 256)
        sg_ref[:, here] = dot(rg[...], w_ref[here, :], NT).astype(BF16)

    p_one = z_rows(0)
    for d in (1, 3, 2):
        arrived("st_p", d, p_in.at[d])
        p_one += p_in[d].astype(F32)
    p_sum[...] = p_one
    at = pl.multiple_of((1 - yh) * 4 * OWN_ROWS, 8)
    mid_out[0] = p_sum[pl.ds(at, 4 * OWN_ROWS), :].astype(BF16)
    copy("mid", 0, mid_out.at[0], mid_in.at[0], y_two).start()

    def q_rows(y):
        pieces = []
        for k in range(4):
            at = pl.multiple_of(k * 2 * OWN_ROWS + y * OWN_ROWS, 8)
            pieces.append(q_sum[pl.ds(at, OWN_ROWS), :])
        return jnp.concatenate(pieces, axis=0)

    q_one = x_rows(0)
    for d in (1, 3, 2):
        arrived("st_q", d, q_in.at[d])
        q_one += q_in[d].astype(F32)
    q_sum[...] = q_one
    mid_out[1] = q_rows(1 - yh).astype(BF16)
    copy("mid", 1, mid_out.at[1], mid_in.at[1], y_two).start()

    arrived("mid", 0, mid_in.at[0])
    at = pl.multiple_of(yh * 4 * OWN_ROWS, 8)
    p_two[...] = p_sum[pl.ds(at, 4 * OWN_ROWS), :] + mid_in[0].astype(F32)

    def end_rows(p, d):
        return pl.ds(pl.multiple_of(lax.rem(p + d, 4) * OWN_ROWS, 8), OWN_ROWS)

    def p_last(d):
        return copy("end_p", d, p_two.at[end_rows(px, d)], p_end.at[d], ring_x(d))

    def q_last(d):
        return copy("end_q", d, q_two.at[end_rows(pz, d)], q_end.at[d], ring_z(d))

    for d in (2, 1, 3):
        p_last(d).start()
    arrived("mid", 1, mid_in.at[1])
    q_two[...] = q_rows(yh) + mid_in[1].astype(F32)
    for d in (2, 1, 3):
        q_last(d).start()

    p_fin = p_two[end_rows(px, 0), :]
    q_fin = q_two[end_rows(pz, 0), :]
    for d in (1, 3, 2):
        arrived("end_p", d, p_end.at[d])
        p_fin += p_end[d]
    for d in (1, 3, 2):
        arrived("end_q", d, q_end.at[d])
        q_fin += q_end[d]
    both = jnp.concatenate([p_fin, q_fin], axis=1)
    first, second = both[:20], both[20:]
    theirs = jnp.where(core == 0, second, first)
    mine = jnp.where(core == 0, first, second)
    last_out[...] = jnp.concatenate([theirs, jnp.zeros((4, HALF), F32)], axis=0)
    copy("last", 0, last_out, last_in, partner).start()
    arrived("last", 0, last_in)
    got = last_in[:20, :]
    pg_ref[:, 0, :HALF] = jnp.where(core == 0, mine, got)
    pg_ref[:, 0, HALF:] = jnp.where(core == 0, got, mine)

    some = blocks.at[0]
    for q in range(QS):
        left("y", q, some.at[rows(q)])
        left("y_back", q, some.at[rows(q)])
        left("rg", q, rg_theirs.at[rows(q)])
    left("y_id", 0, ids.at[0])
    for k in range(2):
        for q in range(QS):
            if k == 0 or q < 6:
                left("ring", 3 * QS * k + q, some.at[rows(0)])
            if k == 0 or q >= 2:
                left("ring", 3 * QS * k + QS + q, some.at[rows(0)])
            left("ring", 3 * QS * k + 2 * QS + q, some.at[rows(0)])
            left("far", QS * k + q, some.at[rows(0)])
            if k == 0 or extra_of(3, q) is None:
                left("to_next", QS * k + q, some.at[rows(0)])
            if k == 0 or extra_of(1, q) is None:
                left("to_prev", QS * k + q, some.at[rows(0)])
    for n in range(6):
        left("ring_id", n, ids.at[0])
    for n in range(4):
        left("core", n, some)
        left("core_id", n, ids.at[0])
        left("part", n, some)
        left("extra", n, some.at[rows(0)])
        left("y_extra", n, some.at[rows(0)])
    left("core_s", 0, s_other)
    for d in (1, 2, 3):
        left("st_p", d, p_out.at[d])
        left("st_q", d, q_out.at[d])
        left("end_p", d, p_end.at[d])
        left("end_q", d, q_end.at[d])
    for n in range(2):
        left("mid", n, mid_out.at[n])
    left("last", 0, last_out)


def local(states, projection, prompt_ids, log_temper, logit_offset):
    vmem = pl.BlockSpec(memory_space=pltpu.VMEM)
    smem = pl.BlockSpec(memory_space=pltpu.SMEM)
    hbm = pl.BlockSpec(memory_space=pl.ANY)
    scratch = [
        ((ROWS, FEAT), BF16),
        ((FEAT, EMB), BF16),
        ((12, ROWS, EMB), BF16),
        ((12, 8, ROWS), jnp.int32),
        ((ROWS, EMB), F32),
        ((ROWS, 128), F32),
        ((4 * ROWS, 8 * ROWS), BF16),
        ((2, 4, ROWS, EMB), F32),
        ((2, 4, ROWS, EMB), BF16),
        ((2, ROWS, EMB), BF16),
        ((2, 2, ROWS, EMB), BF16),
        ((4 * CHUNK, EMB), BF16),
        ((4 * CHUNK, EMB), BF16),
        ((4, ROWS, EMB), BF16),
        ((4, ROWS, EMB), BF16),
        ((ROWS, EMB), BF16),
        ((ROWS, EMB), BF16),
        ((ROWS, EMB), BF16),
        ((2 * ROWS, HALF), BF16),
        ((ROWS, HALF), BF16),
        ((ROWS, FEAT), BF16),
        ((FEAT, 2 * ROWS), BF16),
        ((FEAT, HALF), F32),
        ((4, FEAT_Z, 256), BF16),
        ((4, FEAT_Z, 256), BF16),
        ((4, FEAT_Z, 256), BF16),
        ((4, FEAT_Z, 256), BF16),
        ((FEAT_Z, 256), F32),
        ((FEAT_Z, 256), F32),
        ((2, FEAT_Z // 2, 256), BF16),
        ((2, FEAT_Z // 2, 256), BF16),
        ((FEAT_Z // 2, 256), F32),
        ((FEAT_Z // 2, 256), F32),
        ((4, OWN_ROWS, 256), F32),
        ((4, OWN_ROWS, 256), F32),
        ((24, HALF), F32),
        ((24, HALF), F32),
    ]
    state_grad, owned = pl.pallas_call(
        kernel,
        out_shape=(
            jax.ShapeDtypeStruct((ROWS, FEAT), BF16),
            jax.ShapeDtypeStruct((20, 1, EMB), F32),
        ),
        in_specs=[hbm, hbm, vmem, smem, smem],
        out_specs=(vmem, vmem),
        scratch_shapes=[pltpu.VMEM(shape, kind) for shape, kind in scratch]
        + [pltpu.SemaphoreType.DMA((3,))]
        + [pltpu.SemaphoreType.DMA((Sems.total(),)), pltpu.SemaphoreType.DMA((Sems.total(),))],
        compiler_params=pltpu.CompilerParams(
            collective_id=0, has_side_effects=True, vmem_limit_bytes=60 * 2**20
        ),
        name="contrast",
    )(states[0], projection[0], prompt_ids.reshape(1, ROWS), log_temper, logit_offset)
    return state_grad[None], owned.reshape(1, 20, EMB)


def solution(mesh):
    return jax.shard_map(
        local,
        mesh=mesh,
        in_specs=(P("tower", "batch", None), P("tower", None, None), P("batch"), P(), P()),
        out_specs=(P("tower", "batch", None), P("tower", "batch", None)),
        check_vma=False,
    )
```

time: 103 us -> 102 us (level)
  no operation moved by 1% of the time
where the time goes in v2:
time: 102 us
  Pallas kernels  96.3 us (94%)
  local copies, waits for them, and re-layouts  3.49 us (3%)
  between operations  1.93 us (2%)
    pallas_call x1, Pallas kernels, local(): pl.pallas_call(kernel, out_shape=(jax.ShapeDtypeStruct((ROWS, FEAT), BF16...  96.3 us
    unnamed x2, local copies, waits for them, and re-layouts  3.49 us

profile of v2, /device:TPU:1, one launch (start us, length us, event | category | flops | bytes accessed | tf_op | source)
XLA Modules:
  0.0 101.8 jit_solution(5620047795461971411)
XLA Ops:
  1.9 96.3 %contrast.1 = (bf16[256,1280]{1,0:T(8,128)(2,1)}, f32[20,1,1024]{2,1,0:T(1,128)}) custom-call(bf16[256,1280]{1,0:T(8,128)(2,1)} %bitcast.7, bf16[1280,1024]{1,0:T(8,128)(2,1)} %bitcast.5, s32[1,256]{1,0:T(1,128)} %bitcast.9, f32[1]{0:T(128)S(6)} %copy.9.lt_ref, f32[1]{0:T(128)S(6)} %copy.10.of_ref), custom_call_target="tpu_custom_call" | custom-call | tf_op jit(solution)/shard_map/contrast/pallas_call | solution.py:609
  98.3 2.0 %copy.11 = bf16[1,256,1280]{2,1,0:T(8,128)(2,1)} copy(bf16[1,256,1280]{2,1,0:T(8,128)(2,1)} %bitcast.6) | data formatting | bytes 1310720
  100.2 1.5 %copy.12 = f32[1,20,1024]{2,0,1:T(1,128)} copy(f32[1,20,1024]{2,0,1:T(1,128)} %bitcast.8) | data formatting | bytes 163840

commit v3 on v2

--- a/solution.py
+++ b/solution.py
@@ -25,8 +25,6 @@
 Y_ORDER = (0, 4, 1, 5, 2, 6, 3, 7)
 NEXT_ORDER = (0, 1, 2, 3, 6, 7, 4, 5)
 PREV_ORDER = (4, 5, 6, 7, 0, 1, 2, 3)
-BACK_NEXT = (4, 5, 0, 1, 2, 3, 6, 7)
-BACK_PREV = ((2, 3, 4, 5, 6, 7, 0, 1), (4, 5, 6, 7, 2, 3))
 BACK_ORDER = (4, 5, 6, 0, 7, 1, 2, 3)
 
 
@@ -367,32 +365,6 @@
             out_buf[k, slot, rows(q), :] = term.astype(BF16)
             make(k, q).start()
 
-    other_terms(2)
-    send_far(1)
-
-    @pl.loop(0, 3)
-    def _(u):
-        unit(u + u // 2, 2)
-
-    give(2)
-    other_terms(3)
-    send_extra(3)
-    send_near(1, 3, BACK_NEXT, next_copy)
-    keep(2)
-    send_far(0)
-    other_terms(1)
-    send_extra(1)
-    send_near(1, 1, BACK_PREV[1], prev_copy)
-    give(3)
-    give(1)
-    keep(3)
-    send_near(0, 3, BACK_NEXT, next_copy)
-    keep(1)
-    send_near(0, 1, BACK_PREV[0], prev_copy)
-    other_terms(0)
-    give(0)
-    keep(0)
-
     def reduced(k, q):
         total = grad[k, 0, rows(q), :]
         if k == 0 or extra_of(3, q) is None:
@@ -406,9 +378,46 @@
     def back_copy(q):
         return copy("y_back", q, y_out.at[rows(q)], y_in.at[rows(q)], y_down)
 
-    for q in BACK_ORDER:
-        y_out[rows(q), :] = reduced(1, q).astype(BF16)
-        back_copy(q).start()
+    def send_back(order):
+        for q in order:
+            y_out[rows(q), :] = reduced(1, q).astype(BF16)
+            back_copy(q).start()
+
+    other_terms(2)
+    send_far(1)
+
+    @pl.loop(0, 3)
+    def _(u):
+        unit(u + u // 2, 2)
+
+    give(2)
+    other_terms(3)
+    send_extra(3)
+    send_near(1, 3, (4, 5), next_copy)
+    keep(2)
+    send_far(0)
+    other_terms(1)
+    send_extra(1)
+    send_near(1, 1, (2, 3), prev_copy)
+    send_near(1, 3, (0, 1, 2, 3), next_copy)
+    send_near(1, 1, (4, 5, 6, 7), prev_copy)
+    give(3)
+    give(1)
+    other_terms(0)
+    keep(3)
+    send_near(0, 3, (4, 5), next_copy)
+    keep(1)
+    send_near(0, 1, (2, 3), prev_copy)
+    send_back(BACK_ORDER[:2])
+    for n in range(4):
+        send_near(0, 3, (n,), next_copy)
+        send_near(0, 1, (n + 4,), prev_copy)
+    send_near(0, 3, (6, 7), next_copy)
+    send_near(0, 1, (0, 1), prev_copy)
+    give(0)
+    send_back(BACK_ORDER[2:4])
+    keep(0)
+    send_back(BACK_ORDER[4:])
 
     def rg_copy(q):
         return copy("rg", q, rg_theirs.at[rows(q)], rg_mine.at[pl.ds(ROWS + CHUNK * q, CHUNK)], partner)

time: 102 us -> 94.1 us (0.923)
  Pallas kernels: 96.3 us -> 88.5 us
    pallas_call x1, Pallas kernels: 96.3 us -> 88.5 us  [local(): pl.pallas_call(kernel, out_shape=(jax.ShapeDtypeStruct((ROWS, FEAT), BF16...]
where the time goes in v3:
time: 94.1 us; the launch traced here: 93.9 us
  Pallas kernels  88.5 us (94%)
  local copies, waits for them, and re-layouts  3.49 us (4%)
  between operations  1.93 us (2%)
    pallas_call x1, Pallas kernels, local(): pl.pallas_call(kernel, out_shape=(jax.ShapeDtypeStruct((ROWS, FEAT), BF16...  88.5 us
    unnamed x2, local copies, waits for them, and re-layouts  3.49 us

profile of v3, /device:TPU:1, one launch (start us, length us, event | category | flops | bytes accessed | tf_op | source)
XLA Modules:
  0.0 93.9 jit_solution(16905238140231457356)
XLA Ops:
  1.9 88.5 %contrast.1 = (bf16[256,1280]{1,0:T(8,128)(2,1)}, f32[20,1,1024]{2,1,0:T(1,128)}) custom-call(bf16[256,1280]{1,0:T(8,128)(2,1)} %bitcast.7, bf16[1280,1024]{1,0:T(8,128)(2,1)} %bitcast.5, s32[1,256]{1,0:T(1,128)} %bitcast.9, f32[1]{0:T(128)S(6)} %copy.9.lt_ref, f32[1]{0:T(128)S(6)} %copy.10.of_ref), custom_call_target="tpu_custom_call" | custom-call | tf_op jit(solution)/shard_map/contrast/pallas_call | solution.py:618
  90.4 2.0 %copy.11 = bf16[1,256,1280]{2,1,0:T(8,128)(2,1)} copy(bf16[1,256,1280]{2,1,0:T(8,128)(2,1)} %bitcast.6) | data formatting | bytes 1310720
  92.4 1.5 %copy.12 = f32[1,20,1024]{2,0,1:T(1,128)} copy(f32[1,20,1024]{2,0,1:T(1,128)} %bitcast.8) | data formatting | bytes 163840

commit v4 on v3

--- a/solution.py
+++ b/solution.py
@@ -32,7 +32,7 @@
     sizes = dict(
         y=QS, y_id=1, ring=2 * 3 * QS, ring_id=2 * 3, core=4, core_id=4, core_s=1, extra=4,
         part=4, far=2 * QS, to_next=2 * QS, to_prev=2 * QS, y_extra=4, y_back=QS,
-        rg=QS, st_p=4, st_q=4, mid=2, end_p=4, end_q=4, last=1,
+        rg=QS, st=8, end=16, last=1,
     )
 
     @classmethod
@@ -54,10 +54,10 @@
 
 
 def kernel(
-    s_hbm, w_hbm, id_ref, lt_ref, of_ref, sg_ref, pg_ref,
-    s_ref, w_ref, blocks, ids, raw, inv, pair, grad, out_buf, far_in, near_in, extra_out, extra_in, part_out, part_in, y_out, y_in,
-    rg, rg_mine, rg_theirs, s_other, s_t, mat, p_out, q_out, p_in, q_in, p_sum, q_sum, mid_out, mid_in,
-    p_two, q_two, p_end, q_end, last_out, last_in, lsem, ssem, rsem,
+    s_hbm, w_hbm, id_hbm, lt_hbm, of_hbm, sg_ref, pg_ref,
+    s_ref, w_ref, id_ref, lt_ref, of_ref, blocks, ids, raw, inv, pair, grad, out_buf, far_in, near_in, extra_out, extra_in, part_out, part_in, y_out, y_in,
+    rg, rg_mine, rg_theirs, s_other, s_t, s_x, tall, st_out, st_in, st_sum, end_out, end_in, last_out, last_in,
+    lsem, ssem, rsem,
 ):
     tower = lax.axis_index("tower")
     batch = lax.axis_index("batch")
@@ -83,7 +83,11 @@
     partner = dev(tower, pz, yh, px, 1 - core)
     y_up = dev(other, pz, jnp.where(tower == 1, 1 - yh, yh), px, core)
     y_down = dev(other, pz, jnp.where(tower == 0, 1 - yh, yh), px, core)
-    y_two = dev(tower, pz, 1 - yh, px, core)
+
+    def plane(n, dy, d):
+        x = lax.rem(px + d, 4) if n == 0 else px
+        z = pz if n == 0 else lax.rem(pz + d, 4)
+        return dev(tower, z, 1 - yh if dy else yh, x, core)
 
     def block(k, slot):
         return 2 * slot if k == 0 else OTHER0 + slot
@@ -108,7 +112,8 @@
         return blocks.at[block(k, slot), rows(q)]
 
     barrier = pltpu.get_barrier_semaphore()
-    near = [partner, y_up, y_down, y_two] + [ring_x(d) for d in (1, 2, 3)] + [ring_z(d) for d in (1, 2, 3)]
+    near = [partner, y_up, y_down, plane(0, 1, 0)]
+    near += [plane(n, dy, d) for n in range(2) for dy in range(2) for d in (1, 2, 3)]
     for where in near:
         pl.semaphore_signal(barrier, inc=1, device_id=where, device_id_type=MESH)
 
@@ -117,9 +122,14 @@
 
     loads = [pltpu.make_async_copy(s_hbm, s_ref, lsem.at[0])]
     loads += [pltpu.make_async_copy(w_hbm.at[:, halves(n)], w_ref.at[:, halves(n)], lsem.at[1 + n]) for n in range(2)]
-    for load in loads:
+    small = [(id_hbm, id_ref), (lt_hbm, lt_ref), (of_hbm, of_ref)]
+    small = [pltpu.make_async_copy(src, dst, lsem.at[3 + n]) for n, (src, dst) in enumerate(small)]
+    for load in loads + small:
         load.start()
+    small[0].wait()
     ids[0] = jnp.broadcast_to(id_ref[...], (8, ROWS))
+    small[1].wait()
+    small[2].wait()
     loads[0].wait()
     for n in range(2):
         loads[1 + n].wait()
@@ -187,8 +197,16 @@
     for q in (7, 0, 1, 2, 3):
         to_prev(0, q).start()
     core_send(0)
+    def turn(states, first):
+        tall[...] = states[...].astype(F32).T
+        here = pl.ds(first, ROWS)
+        s_t[:, here] = tall[...].astype(BF16)
+        for x in range(4):
+            pieces = [tall[pl.ds((4 * k + x) * OWN_ROWS, OWN_ROWS), :] for k in range(8)]
+            s_x[pl.ds(x * FEAT_Z, FEAT_Z), here] = jnp.concatenate(pieces, axis=0).astype(BF16)
+
     copy("core_s", 0, s_ref, s_other, partner).start()
-    s_t[:, :ROWS] = s_ref[...].T
+    turn(s_ref, 0)
 
     def step(m):
         q = Y_ORDER[m]
@@ -224,7 +242,7 @@
     arrived("y_id", 0, ids.at[OTHER0])
     ids_out(1)
     arrived("core_s", 0, s_other)
-    s_t[:, ROWS:] = s_other[...].T
+    turn(s_other, ROWS)
     step(2)
     step(3)
     pass_next(0)
@@ -439,91 +457,53 @@
     for q in range(QS):
         arrived("rg", q, rg_mine.at[pl.ds(ROWS + CHUNK * q, CHUNK)])
 
-    @pl.loop(0, FEAT // 256)
-    def _(n):
-        here = pl.ds(pl.multiple_of(n * 256, 256), 256)
-        mat[here, :] = dot(s_t[here, :], rg_mine[...], NN)
-
-    def z_rows(d):
-        at = pl.ds(pl.multiple_of(lax.rem(pz + d, 4) * FEAT_Z, FEAT_Z), FEAT_Z)
-        return mat[at, :256]
-
-    def x_rows(d):
-        pieces = []
-        for k in range(8):
-            at = pl.multiple_of(k * 4 * OWN_ROWS + lax.rem(px + d, 4) * OWN_ROWS, 8)
-            pieces.append(mat[pl.ds(at, OWN_ROWS), 256:])
-        return jnp.concatenate(pieces, axis=0)
-
-    def p_copy(d):
-        return copy("st_p", d, p_out.at[d], p_in.at[d], ring_z(d))
-
-    def q_copy(d):
-        return copy("st_q", d, q_out.at[d], q_in.at[d], ring_x(d))
+    def part_of(n, d):
+        at = pl.multiple_of(lax.rem((px if n else pz) + d, 4) * FEAT_Z, FEAT_Z)
+        return dot((s_x if n else s_t)[pl.ds(at, FEAT_Z), :], rg_mine[:, pl.ds(256 * n, 256)], NN)
+
+    def st_copy(n, d):
+        return copy("st", 4 * n + d, st_out.at[n, d], st_in.at[n, d], ring_x(d) if n else ring_z(d))
 
     for d in (2, 1, 3):
-        p_out[d] = z_rows(d).astype(BF16)
-        p_copy(d).start()
-        q_out[d] = x_rows(d).astype(BF16)
-        q_copy(d).start()
+        for n in range(2):
+            st_out[n, d] = part_of(n, d).astype(BF16)
+            st_copy(n, d).start()
+    for n in range(2):
+        st_sum[n] = part_of(n, 0)
 
     @pl.loop(0, FEAT // 256)
     def _(n):
         here = pl.ds(pl.multiple_of(n * 256, 256), 256)
         sg_ref[:, here] = dot(rg[...], w_ref[here, :], NT).astype(BF16)
 
-    p_one = z_rows(0)
-    for d in (1, 3, 2):
-        arrived("st_p", d, p_in.at[d])
-        p_one += p_in[d].astype(F32)
-    p_sum[...] = p_one
-    at = pl.multiple_of((1 - yh) * 4 * OWN_ROWS, 8)
-    mid_out[0] = p_sum[pl.ds(at, 4 * OWN_ROWS), :].astype(BF16)
-    copy("mid", 0, mid_out.at[0], mid_in.at[0], y_two).start()
-
-    def q_rows(y):
-        pieces = []
-        for k in range(4):
-            at = pl.multiple_of(k * 2 * OWN_ROWS + y * OWN_ROWS, 8)
-            pieces.append(q_sum[pl.ds(at, OWN_ROWS), :])
-        return jnp.concatenate(pieces, axis=0)
-
-    q_one = x_rows(0)
-    for d in (1, 3, 2):
-        arrived("st_q", d, q_in.at[d])
-        q_one += q_in[d].astype(F32)
-    q_sum[...] = q_one
-    mid_out[1] = q_rows(1 - yh).astype(BF16)
-    copy("mid", 1, mid_out.at[1], mid_in.at[1], y_two).start()
-
-    arrived("mid", 0, mid_in.at[0])
-    at = pl.multiple_of(yh * 4 * OWN_ROWS, 8)
-    p_two[...] = p_sum[pl.ds(at, 4 * OWN_ROWS), :] + mid_in[0].astype(F32)
-
-    def end_rows(p, d):
-        return pl.ds(pl.multiple_of(lax.rem(p + d, 4) * OWN_ROWS, 8), OWN_ROWS)
-
-    def p_last(d):
-        return copy("end_p", d, p_two.at[end_rows(px, d)], p_end.at[d], ring_x(d))
-
-    def q_last(d):
-        return copy("end_q", d, q_two.at[end_rows(pz, d)], q_end.at[d], ring_z(d))
-
-    for d in (2, 1, 3):
-        p_last(d).start()
-    arrived("mid", 1, mid_in.at[1])
-    q_two[...] = q_rows(yh) + mid_in[1].astype(F32)
-    for d in (2, 1, 3):
-        q_last(d).start()
-
-    p_fin = p_two[end_rows(px, 0), :]
-    q_fin = q_two[end_rows(pz, 0), :]
-    for d in (1, 3, 2):
-        arrived("end_p", d, p_end.at[d])
-        p_fin += p_end[d]
-    for d in (1, 3, 2):
-        arrived("end_q", d, q_end.at[d])
-        q_fin += q_end[d]
+    def group(n, dy, d):
+        y = jnp.where(dy == 0, yh, 1 - yh)
+        g = y * 4 + lax.rem(px + d, 4) if n == 0 else lax.rem(pz + d, 4) * 2 + y
+        return st_sum[n, pl.ds(pl.multiple_of(g * OWN_ROWS, 8), OWN_ROWS), :]
+
+    def stacked(value):
+        return jnp.concatenate([value[:, :128], value[:, 128:]], axis=0)
+
+    def end_copy(n, k):
+        return copy("end", 8 * n + k, end_out.at[n, k], end_in.at[n, k], plane(n, k // 4, k % 4))
+
+    for n in range(2):
+        for d in (1, 3, 2):
+            arrived("st", 4 * n + d, st_in.at[n, d])
+        st_sum[n] += st_in[n, 1].astype(F32) + st_in[n, 2].astype(F32) + st_in[n, 3].astype(F32)
+        for k in (6, 5, 7, 4, 2, 1, 3):
+            end_out[n, k] = stacked(group(n, k // 4, k % 4)).astype(BF16)
+            end_copy(n, k).start()
+
+    def finished(n):
+        total = stacked(group(n, 0, 0))
+        for k in (1, 3, 2, 4, 5, 7, 6):
+            arrived("end", 8 * n + k, end_in.at[n, k])
+            total += end_in[n, k].astype(F32)
+        return jnp.concatenate([total[:OWN_ROWS], total[OWN_ROWS:]], axis=1)
+
+    p_fin = finished(0)
+    q_fin = finished(1)
     both = jnp.concatenate([p_fin, q_fin], axis=1)
     first, second = both[:20], both[20:]
     theirs = jnp.where(core == 0, second, first)
@@ -562,23 +542,23 @@
         left("extra", n, some.at[rows(0)])
         left("y_extra", n, some.at[rows(0)])
     left("core_s", 0, s_other)
-    for d in (1, 2, 3):
-        left("st_p", d, p_out.at[d])
-        left("st_q", d, q_out.at[d])
-        left("end_p", d, p_end.at[d])
-        left("end_q", d, q_end.at[d])
     for n in range(2):
-        left("mid", n, mid_out.at[n])
+        for d in (1, 2, 3):
+            left("st", 4 * n + d, st_out.at[n, d])
+        for k in range(1, 8):
+            left("end", 8 * n + k, end_out.at[n, k])
     left("last", 0, last_out)
 
 
 def local(states, projection, prompt_ids, log_temper, logit_offset):
     vmem = pl.BlockSpec(memory_space=pltpu.VMEM)
-    smem = pl.BlockSpec(memory_space=pltpu.SMEM)
     hbm = pl.BlockSpec(memory_space=pl.ANY)
     scratch = [
         ((ROWS, FEAT), BF16),
         ((FEAT, EMB), BF16),
+        ((1, ROWS), jnp.int32),
+        None,
+        None,
         ((12, ROWS, EMB), BF16),
         ((12, 8, ROWS), jnp.int32),
         ((ROWS, EMB), F32),
@@ -599,19 +579,13 @@
         ((ROWS, HALF), BF16),
         ((ROWS, FEAT), BF16),
         ((FEAT, 2 * ROWS), BF16),
-        ((FEAT, HALF), F32),
-        ((4, FEAT_Z, 256), BF16),
-        ((4, FEAT_Z, 256), BF16),
-        ((4, FEAT_Z, 256), BF16),
-        ((4, FEAT_Z, 256), BF16),
-        ((FEAT_Z, 256), F32),
-        ((FEAT_Z, 256), F32),
-        ((2, FEAT_Z // 2, 256), BF16),
-        ((2, FEAT_Z // 2, 256), BF16),
-        ((FEAT_Z // 2, 256), F32),
-        ((FEAT_Z // 2, 256), F32),
-        ((4, OWN_ROWS, 256), F32),
-        ((4, OWN_ROWS, 256), F32),
+        ((FEAT, 2 * ROWS), BF16),
+        ((FEAT, ROWS), F32),
+        ((2, 4, FEAT_Z, 256), BF16),
+        ((2, 4, FEAT_Z, 256), BF16),
+        ((2, FEAT_Z, 256), F32),
+        ((2, 8, 2 * OWN_ROWS, 128), BF16),
+        ((2, 8, 2 * OWN_ROWS, 128), BF16),
         ((24, HALF), F32),
         ((24, HALF), F32),
     ]
@@ -621,10 +595,10 @@
             jax.ShapeDtypeStruct((ROWS, FEAT), BF16),
             jax.ShapeDtypeStruct((20, 1, EMB), F32),
         ),
-        in_specs=[hbm, hbm, vmem, smem, smem],
+        in_specs=[hbm] * 5,
         out_specs=(vmem, vmem),
-        scratch_shapes=[pltpu.VMEM(shape, kind) for shape, kind in scratch]
-        + [pltpu.SemaphoreType.DMA((3,))]
+        scratch_shapes=[pltpu.VMEM(*what) if what else pltpu.SMEM((1,), F32) for what in scratch]
+        + [pltpu.SemaphoreType.DMA((6,))]
         + [pltpu.SemaphoreType.DMA((Sems.total(),)), pltpu.SemaphoreType.DMA((Sems.total(),))],
         compiler_params=pltpu.CompilerParams(
             collective_id=0, has_side_effects=True, vmem_limit_bytes=60 * 2**20

time: 94.1 us -> 89.7 us (0.953)
  Pallas kernels: 88.5 us -> 84 us
    pallas_call x1, Pallas kernels: 88.5 us -> 84 us  [local(): pl.pallas_call(kernel, out_shape=(jax.ShapeDtypeStruct((ROWS, FEAT), BF16...]
where the time goes in v4:
time: 89.7 us; the launch traced here: 89.5 us
  Pallas kernels  84 us (94%)
  local copies, waits for them, and re-layouts  3.49 us (4%)
  between operations  1.93 us (2%)
    pallas_call x1, Pallas kernels, local(): pl.pallas_call(kernel, out_shape=(jax.ShapeDtypeStruct((ROWS, FEAT), BF16...  84 us
    unnamed x2, local copies, waits for them, and re-layouts  3.49 us

profile of v4, /device:TPU:1, one launch (start us, length us, event | category | flops | bytes accessed | tf_op | source)
XLA Modules:
  0.0 89.5 jit_solution(16406337736250615348)
XLA Ops:
  1.9 84.0 %contrast.1 = (bf16[256,1280]{1,0:T(8,128)(2,1)}, f32[20,1,1024]{2,1,0:T(1,128)}) custom-call(bf16[256,1280]{1,0:T(8,128)(2,1)} %bitcast.7, bf16[1280,1024]{1,0:T(8,128)(2,1)} %bitcast.5, s32[1,256]{1,0:T(1,128)} %bitcast.9, f32[1]{0:T(128)S(6)} %copy.9.lt_hbm, f32[1]{0:T(128)S(6)} %copy.10.of_hbm), custom_call_target="tpu_custom_call" | custom-call | tf_op jit(solution)/shard_map/contrast/pallas_call | solution.py:592
  86.0 2.0 %copy.11 = bf16[1,256,1280]{2,1,0:T(8,128)(2,1)} copy(bf16[1,256,1280]{2,1,0:T(8,128)(2,1)} %bitcast.6) | data formatting | bytes 1310720
  87.9 1.5 %copy.12 = f32[1,20,1024]{2,0,1:T(1,128)} copy(f32[1,20,1024]{2,0,1:T(1,128)} %bitcast.8) | data formatting | bytes 163840

commit v5 on v4

--- a/solution.py
+++ b/solution.py
@@ -23,14 +23,15 @@
 OTHER0 = 8
 
 Y_ORDER = (0, 4, 1, 5, 2, 6, 3, 7)
-NEXT_ORDER = (0, 1, 2, 3, 6, 7, 4, 5)
-PREV_ORDER = (4, 5, 6, 7, 0, 1, 2, 3)
+NEXT_ORDER = (2, 3, 0, 1, 6, 7, 4, 5)
+PREV_ORDER = (6, 7, 4, 5, 2, 3, 0, 1)
+EXTRA = (2, 6, 3, 7)
 BACK_ORDER = (4, 5, 6, 0, 7, 1, 2, 3)
 
 
 class Sems:
     sizes = dict(
-        y=QS, y_id=1, ring=2 * 3 * QS, ring_id=2 * 3, core=4, core_id=4, core_s=1, extra=4,
+        y=QS, y_id=1, ring=2 * 3 * QS, ring_id=2 * 3, core=16, core_id=4, core_s=1, extra=4,
         part=4, far=2 * QS, to_next=2 * QS, to_prev=2 * QS, y_extra=4, y_back=QS,
         rg=QS, st=8, end=16, last=1,
     )
@@ -157,12 +158,7 @@
         arrived("ring", 3 * QS * k + 2 * QS + q, piece(k, 2, q))
 
     def extra(n):
-        slot, q = ((1, 6), (1, 7), (3, 0), (3, 1))[n]
-        return copy("extra", n, piece(0, slot, q), piece(1, slot, q), y_up)
-
-    def got_extra(n):
-        slot, q = ((1, 6), (1, 7), (3, 0), (3, 1))[n]
-        arrived("extra", n, piece(1, slot, q))
+        return copy("extra", n, piece(0, 2, EXTRA[n]), piece(1, 2, EXTRA[n]), y_up)
 
     def ids_out(k):
         copy("ring_id", 3 * k, ids.at[block(k, 0)], ids.at[block(k, 1)], ring(k, 1)).start()
@@ -173,30 +169,52 @@
         copy("ring_id", 3 * k + 2, ids.at[block(k, 1)], ids.at[block(k, 2)], ring(k, 1)).start()
         arrived("ring_id", 3 * k + 1, ids.at[block(k, 3)])
 
-    def core_send(slot):
-        copy("core", slot, blocks.at[2 * slot], blocks.at[2 * slot + 1], partner).start()
+    def core_copy(slot, n):
+        there = pl.ds(2 * CHUNK * n, 2 * CHUNK)
+        return copy("core", 4 * slot + n, blocks.at[2 * slot, there], blocks.at[2 * slot + 1, there], partner)
+
+    def core_send(slot, *pieces):
+        for n in pieces:
+            core_copy(slot, n).start()
+
+    def core_got(slot):
+        for n in range(4):
+            arrived("core", 4 * slot + n, blocks.at[2 * slot + 1, pl.ds(2 * CHUNK * n, 2 * CHUNK)])
+        arrived("core_id", slot, ids.at[2 * slot + 1])
+
+    def core_ids(slot):
         copy("core_id", slot, ids.at[2 * slot], ids.at[2 * slot + 1], partner).start()
-
-    def core_got(slot):
-        arrived("core", slot, blocks.at[2 * slot + 1])
-        arrived("core_id", slot, ids.at[2 * slot + 1])
 
     copy("y_id", 0, ids.at[0], ids.at[OTHER0], y_up).start()
     ids_out(0)
-    for m, q in enumerate(Y_ORDER):
+    def own_rows(q):
         part = raw[rows(q), :]
         length = jnp.sqrt(jnp.sum(part * part, axis=1, keepdims=True) + EPSILON)
         scale = 1.0 / length
         inv[rows(q), :] = jnp.broadcast_to(scale, (CHUNK, 128))
         blocks[0, rows(q)] = (part * scale).astype(BF16)
+
+    def y_send(q):
         copy("y", q, piece(0, 0, q), piece(1, 0, q), y_up).start()
-        if m < 6:
-            (to_next(0, q) if q < 4 else to_prev(0, q)).start()
-    for q in (3, 6, 7, 4, 5):
+
+    for q in (0, 1):
+        own_rows(q)
+        y_send(q)
+        own_rows(q + 2)
+        to_next(0, q + 2).start()
+        own_rows(q + 4)
+        y_send(q + 4)
+        own_rows(q + 6)
+        to_prev(0, q + 6).start()
+    for q in EXTRA:
+        y_send(q)
+    for q in (0, 1, 6):
         to_next(0, q).start()
-    for q in (7, 0, 1, 2, 3):
+    for q in (4, 5, 2):
         to_prev(0, q).start()
-    core_send(0)
+    core_send(0, 0, 1, 2, 3)
+    core_ids(0)
+
     def turn(states, first):
         tall[...] = states[...].astype(F32).T
         here = pl.ds(first, ROWS)
@@ -208,65 +226,12 @@
     copy("core_s", 0, s_ref, s_other, partner).start()
     turn(s_ref, 0)
 
-    def step(m):
-        q = Y_ORDER[m]
-        arrived("y", q, piece(1, 0, q))
-        if q < 6:
-            to_next(1, q).start()
-        if q >= 2:
-            to_prev(1, q).start()
-        q = NEXT_ORDER[m]
-        got_next(0, q)
-        if q < 4:
-            onward(0, q).start()
-        elif q >= 6:
-            extra(q - 6).start()
-        q = PREV_ORDER[m]
-        got_prev(0, q)
-        if q >= 4:
-            onward(0, q).start()
-        elif q < 2:
-            extra(2 + q).start()
-
-    def pass_next(q):
-        got_next(1, q)
-        onward(1, q).start()
-
-    def pass_prev(q):
-        got_prev(1, q)
-        onward(1, q).start()
-
-    step(0)
-    step(1)
-    ids_onward(0)
-    arrived("y_id", 0, ids.at[OTHER0])
-    ids_out(1)
-    arrived("core_s", 0, s_other)
-    turn(s_other, ROWS)
-    step(2)
-    step(3)
-    pass_next(0)
-    step(4)
-    pass_prev(4)
-    step(5)
-    pass_next(1)
-    step(6)
-    pass_prev(5)
-    step(7)
-    core_send(1)
-    core_send(3)
-    ids_onward(1)
-    pass_next(2)
-    core_got(0)
-    core_got(1)
-    core_got(3)
-
     temper = jnp.exp(jnp.full((1, 1), lt_ref[0], F32))
     slope = 0.5 * temper
     shift = jnp.full((1, 1), 0.5 * of_ref[0], F32)
 
     def unit(a, b):
-        at = pl.multiple_of(2 * b, 2)
+        at = 2 * b
         own = blocks[pl.ds(at, 2)].reshape(2 * ROWS, EMB)
         logit = dot(blocks[OTHER0 + a], own, NT)
         value = jnp.tanh(logit * slope + shift) * 8.0
@@ -274,70 +239,122 @@
         col = jnp.broadcast_to(ids[OTHER0 + a, 0:1, :].astype(F32), (128, ROWS)).T
         same = jnp.concatenate([col] * 4, axis=1) == row
         value = value + jnp.where(same, -8.0, 8.0)
-        here = pl.ds(pl.multiple_of(a * ROWS, ROWS), ROWS)
-        pair[here, pl.ds(pl.multiple_of(b * 2 * ROWS, 2 * ROWS), 2 * ROWS)] = value.astype(BF16)
-
-    @pl.loop(0, 3)
-    def _(u):
-        unit(0, u + u // 2)
-
-        @pl.when(u == 0)
-        def _():
-            pass_prev(6)
-
-        @pl.when(u == 1)
-        def _():
-            pass_next(3)
-
-        @pl.when(u == 2)
-        def _():
-            pass_prev(7)
-
+        pair[pl.ds(a * ROWS, ROWS), pl.ds(b * 2 * ROWS, 2 * ROWS)] = value.astype(BF16)
+
+    def y_got(m):
+        q = Y_ORDER[m]
+        arrived("y", q, piece(1, 0, q))
+        to_next(1, q).start()
+        to_prev(1, q).start()
+
+    def own_on(m):
+        for q, got in ((NEXT_ORDER[m], got_next), (PREV_ORDER[m], got_prev)):
+            got(0, q)
+            onward(0, q).start()
+
+    def other_on(q):
+        (got_next if q < 4 else got_prev)(1, q)
+        onward(1, q).start()
+
+    def far_on(n):
+        got_onward(0, EXTRA[n])
+        extra(n).start()
+
+    y_got(0)
+    own_on(0)
+    y_got(1)
+    own_on(1)
+    ids_onward(0)
+    core_ids(1)
+    core_ids(3)
+    arrived("y_id", 0, ids.at[OTHER0])
+    ids_out(1)
+    arrived("core_s", 0, s_other)
+    turn(s_other, ROWS)
+    y_got(2)
+    own_on(2)
+    y_got(3)
+    own_on(3)
+    for q in (7, 4, 5):
+        to_next(0, q).start()
+    for q in (3, 0, 1):
+        to_prev(0, q).start()
+    core_send(1, 0, 1)
+    core_send(3, 2, 3)
+    other_on(0)
+    y_got(4)
+    other_on(4)
+    y_got(5)
+    far_on(0)
+    far_on(1)
+    ids_onward(1)
+    other_on(1)
+    y_got(6)
+    far_on(2)
+    far_on(3)
+    core_send(2, 1, 3)
+    other_on(5)
+    y_got(7)
+    arrived("ring_id", 2, ids.at[block(0, 2)])
+    core_ids(2)
+    core_got(0)
+    unit(0, 0)
+    for q in (0, 4):
+        got_onward(0, q)
+    for q in (1, 5):
+        got_onward(0, q)
+    core_send(2, 0, 2)
+    got_next(0, 6)
+    got_next(0, 7)
+    core_send(1, 3)
+    got_prev(0, 2)
+    got_prev(0, 3)
+    core_send(3, 1)
+    core_got(2)
+    unit(0, 2)
     for q in (4, 5):
-        got_next(1, q)
-    for q in (2, 3):
-        got_prev(1, q)
+        got_next(0, q)
+    core_send(1, 2)
+    for q in (0, 1):
+        got_prev(0, q)
+    core_send(3, 0)
+    for q in (0, 4, 1, 5):
+        got_onward(1, q)
     for n in range(4):
-        got_extra(n)
-    for q in range(QS):
-        got_onward(0, q)
-    arrived("ring_id", 2, ids.at[block(0, 2)])
-    core_send(2)
-
-    @pl.loop(0, 6)
-    def _(u):
-        a = u // 3
-        b = u - 3 * a
-        unit(1 + 2 * a, b + b // 2)
-
-    core_got(2)
-    for q in range(QS):
-        got_onward(1, q)
+        arrived("extra", n, piece(1, 2, EXTRA[n]))
     arrived("ring_id", 5, ids.at[block(1, 2)])
-
-    @pl.loop(0, 4)
-    def _(u):
-        unit(2, u)
+    unit(2, 0)
+    unit(2, 2)
+    core_got(1)
+    unit(2, 1)
+    core_got(3)
+    unit(2, 3)
 
     def own_terms(half, slot):
         rest = blocks[pl.ds(OTHER0, 4)].reshape(4 * ROWS, EMB)
         return dot(pair[:, pl.ds((2 * slot + half) * ROWS, ROWS)], rest, TN)
 
     def other_terms(slot):
-        @pl.loop(0, 2)
-        def _(n):
-            cols = pl.ds(pl.multiple_of(n * HALF, HALF), HALF)
+        for n in range(2):
+            cols = halves(n)
             own = blocks[pl.ds(0, 8), :, cols].reshape(8 * ROWS, HALF)
-            grad[1, slot, :, cols] = dot(pair[pl.ds(slot * ROWS, ROWS), :], own, NN)
+            value = dot(pair[pl.ds(slot * ROWS, ROWS), :], own, NN)
+            if slot == 2:
+                out_buf[1, 2, :, cols] = value.astype(BF16)
+            else:
+                grad[1, slot, :, cols] = value
 
     def give(slot):
         part_out[slot] = own_terms(1, slot).astype(BF16)
         copy("part", slot, part_out.at[slot], part_in.at[slot], partner).start()
 
     def keep(slot):
-        grad[0, slot] = own_terms(0, slot)
         arrived("part", slot, part_in.at[slot])
-        grad[0, slot] += part_in[slot].astype(F32)
+        value = own_terms(0, slot) + part_in[slot].astype(F32)
+        if slot == 2:
+            out_buf[0, 2] = value.astype(BF16)
+        else:
+            grad[0, slot] = value
 
     def far_copy(k, q):
         return copy("far", QS * k + q, out_buf.at[k, 2, rows(q)], far_in.at[k, rows(q)], ring(k, 1 if q < 4 else 3))
@@ -358,7 +375,6 @@
 
     def send_far(k):
         for q in (0, 4, 1, 5, 2, 6, 3, 7):
-            out_buf[k, 2, rows(q), :] = grad[k, 2, rows(q), :].astype(BF16)
             far_copy(k, q).start()
 
     def send_extra(slot):
@@ -403,22 +419,33 @@
 
     other_terms(2)
     send_far(1)
-
-    @pl.loop(0, 3)
-    def _(u):
-        unit(u + u // 2, 2)
-
+    for q in (2, 6, 3, 7):
+        got_next(1, q)
+    for q in (5, 4):
+        got_next(1, q)
+    for q in (0, 1, 2, 3, 6, 7):
+        got_prev(1, q)
+    unit(3, 2)
+    unit(1, 2)
     give(2)
+    unit(3, 0)
+    unit(3, 1)
+    unit(3, 3)
     other_terms(3)
     send_extra(3)
     send_near(1, 3, (4, 5), next_copy)
     keep(2)
     send_far(0)
+    unit(1, 0)
+    unit(1, 1)
+    unit(1, 3)
     other_terms(1)
     send_extra(1)
     send_near(1, 1, (2, 3), prev_copy)
     send_near(1, 3, (0, 1, 2, 3), next_copy)
     send_near(1, 1, (4, 5, 6, 7), prev_copy)
+    unit(0, 1)
+    unit(0, 3)
     give(3)
     give(1)
     other_terms(0)
@@ -433,9 +460,9 @@
     send_near(0, 3, (6, 7), next_copy)
     send_near(0, 1, (0, 1), prev_copy)
     give(0)
-    send_back(BACK_ORDER[2:4])
+    send_back(BACK_ORDER[2:6])
     keep(0)
-    send_back(BACK_ORDER[4:])
+    send_back(BACK_ORDER[6:])
 
     def rg_copy(q):
         return copy("rg", q, rg_theirs.at[rows(q)], rg_mine.at[pl.ds(ROWS + CHUNK * q, CHUNK)], partner)
@@ -523,11 +550,10 @@
     left("y_id", 0, ids.at[0])
     for k in range(2):
         for q in range(QS):
-            if k == 0 or q < 6:
-                left("ring", 3 * QS * k + q, some.at[rows(0)])
-            if k == 0 or q >= 2:
-                left("ring", 3 * QS * k + QS + q, some.at[rows(0)])
-            left("ring", 3 * QS * k + 2 * QS + q, some.at[rows(0)])
+            left("ring", 3 * QS * k + q, some.at[rows(0)])
+            left("ring", 3 * QS * k + QS + q, some.at[rows(0)])
+            if k == 0 or q not in EXTRA:
+                left("ring", 3 * QS * k + 2 * QS + q, some.at[rows(0)])
             left("far", QS * k + q, some.at[rows(0)])
             if k == 0 or extra_of(3, q) is None:
                 left("to_next", QS * k + q, some.at[rows(0)])
@@ -536,7 +562,8 @@
     for n in range(6):
         left("ring_id", n, ids.at[0])
     for n in range(4):
-        left("core", n, some)
+        for m in range(4):
+            left("core", 4 * n + m, some.at[pl.ds(0, 2 * CHUNK)])
         left("core_id", n, ids.at[0])
         left("part", n, some)
         left("extra", n, some.at[rows(0)])

time: 89.7 us -> 87.2 us (0.972)
  Pallas kernels: 84 us -> 81.5 us
    pallas_call x1, Pallas kernels: 84 us -> 81.5 us  [local(): pl.pallas_call(kernel, out_shape=(jax.ShapeDtypeStruct((ROWS, FEAT), BF16...]
where the time goes in v5:
time: 87.2 us; the launch traced here: 86.9 us
  Pallas kernels  81.5 us (93%)
  local copies, waits for them, and re-layouts  3.49 us (4%)
  between operations  1.93 us (2%)
    pallas_call x1, Pallas kernels, local(): pl.pallas_call(kernel, out_shape=(jax.ShapeDtypeStruct((ROWS, FEAT), BF16...  81.5 us
    unnamed x2, local copies, waits for them, and re-layouts  3.49 us

profile of v5, /device:TPU:1, one launch (start us, length us, event | category | flops | bytes accessed | tf_op | source)
XLA Modules:
  0.0 86.9 jit_solution(17621864780631140222)
XLA Ops:
  1.9 81.5 %contrast.1 = (bf16[256,1280]{1,0:T(8,128)(2,1)}, f32[20,1,1024]{2,1,0:T(1,128)}) custom-call(bf16[256,1280]{1,0:T(8,128)(2,1)} %bitcast.7, bf16[1280,1024]{1,0:T(8,128)(2,1)} %bitcast.5, s32[1,256]{1,0:T(1,128)} %bitcast.9, f32[1]{0:T(128)S(6)} %copy.9.lt_hbm, f32[1]{0:T(128)S(6)} %copy.10.of_hbm), custom_call_target="tpu_custom_call" | custom-call | tf_op jit(solution)/shard_map/contrast/pallas_call | solution.py:619
  83.5 2.0 %copy.11 = bf16[1,256,1280]{2,1,0:T(8,128)(2,1)} copy(bf16[1,256,1280]{2,1,0:T(8,128)(2,1)} %bitcast.6) | data formatting | bytes 1310720
  85.4 1.5 %copy.12 = f32[1,20,1024]{2,0,1:T(1,128)} copy(f32[1,20,1024]{2,0,1:T(1,128)} %bitcast.8) | data formatting | bytes 163840

commit v6 on v5

--- a/solution.py
+++ b/solution.py
@@ -18,6 +18,7 @@
 CHUNK = 32
 QS = ROWS // CHUNK
 HALF = EMB // 2
+QUARTERS = 4
 FEAT_Z = FEAT // 4
 OWN_ROWS = 40
 OTHER0 = 8
@@ -55,8 +56,8 @@
 
 
 def kernel(
-    s_hbm, w_hbm, id_hbm, lt_hbm, of_hbm, sg_ref, pg_ref,
-    s_ref, w_ref, id_ref, lt_ref, of_ref, blocks, ids, raw, inv, pair, grad, out_buf, far_in, near_in, extra_out, extra_in, part_out, part_in, y_out, y_in,
+    s_hbm, w_hbm, id_hbm, lt_hbm, of_hbm, sg_hbm, pg_ref,
+    s_ref, w_ref, cols, sg_ref, id_ref, lt_ref, of_ref, blocks, ids, raw, inv, pair, grad, out_buf, far_in, near_in, extra_out, extra_in, part_out, part_in, y_out, y_in,
     rg, rg_mine, rg_theirs, s_other, s_t, s_x, tall, st_out, st_in, st_sum, end_out, end_in, last_out, last_in,
     lsem, ssem, rsem,
 ):
@@ -121,10 +122,13 @@
     def halves(n):
         return pl.ds(n * HALF, HALF)
 
+    def quarter(n):
+        return pl.ds(n * (EMB // QUARTERS), EMB // QUARTERS)
+
     loads = [pltpu.make_async_copy(s_hbm, s_ref, lsem.at[0])]
-    loads += [pltpu.make_async_copy(w_hbm.at[:, halves(n)], w_ref.at[:, halves(n)], lsem.at[1 + n]) for n in range(2)]
+    loads += [pltpu.make_async_copy(w_hbm.at[:, quarter(n)], w_ref.at[:, quarter(n)], lsem.at[1 + n]) for n in range(QUARTERS)]
     small = [(id_hbm, id_ref), (lt_hbm, lt_ref), (of_hbm, of_ref)]
-    small = [pltpu.make_async_copy(src, dst, lsem.at[3 + n]) for n, (src, dst) in enumerate(small)]
+    small = [pltpu.make_async_copy(src, dst, lsem.at[1 + QUARTERS + n]) for n, (src, dst) in enumerate(small)]
     for load in loads + small:
         load.start()
     small[0].wait()
@@ -132,9 +136,9 @@
     small[1].wait()
     small[2].wait()
     loads[0].wait()
-    for n in range(2):
+    for n in range(QUARTERS):
         loads[1 + n].wait()
-        raw[:, halves(n)] = dot(s_ref[...], w_ref[:, halves(n)], NN)
+        raw[:, quarter(n)] = dot(s_ref[...], w_ref[:, quarter(n)], NN)
 
     pl.semaphore_wait(barrier, len(near))
 
@@ -177,9 +181,11 @@
         for n in pieces:
             core_copy(slot, n).start()
 
-    def core_got(slot):
-        for n in range(4):
+    def core_got(slot, *pieces):
+        for n in pieces:
             arrived("core", 4 * slot + n, blocks.at[2 * slot + 1, pl.ds(2 * CHUNK * n, 2 * CHUNK)])
+
+    def core_ids_got(slot):
         arrived("core_id", slot, ids.at[2 * slot + 1])
 
     def core_ids(slot):
@@ -230,16 +236,44 @@
     slope = 0.5 * temper
     shift = jnp.full((1, 1), 0.5 * of_ref[0], F32)
 
+    def id_columns(slot):
+        cols[slot] = jnp.broadcast_to(ids[OTHER0 + slot, 0:1, :].astype(F32), (128, ROWS)).T
+
+    other_rows = {
+        "0": [(0, 0, 256)],
+        "2": [(2, 0, 256)],
+        "early": [(1, 0, 64), (1, 128, 64), (3, 0, 64), (3, 128, 64)],
+        "late": [(1, 64, 64), (1, 192, 64), (3, 64, 64), (3, 192, 64)],
+    }
+    own_rows_of = {
+        "0": [(0, 0, 0, 256), (0, 1, 0, 256)],
+        "2": [(2, 0, 0, 256), (2, 1, 0, 256)],
+        "early": [(1, 0, 0, 128), (1, 1, 0, 128), (3, 0, 128, 128), (3, 1, 128, 128)],
+        "late": [(1, 0, 128, 128), (1, 1, 128, 128), (3, 0, 0, 128), (3, 1, 0, 128)],
+    }
+
+    def joined(parts, axis):
+        return parts[0] if len(parts) == 1 else jnp.concatenate(parts, axis=axis)
+
     def unit(a, b):
-        at = 2 * b
-        own = blocks[pl.ds(at, 2)].reshape(2 * ROWS, EMB)
-        logit = dot(blocks[OTHER0 + a], own, NT)
+        left_side, right_side = other_rows[a], own_rows_of[b]
+        rest = joined([blocks[OTHER0 + n, pl.ds(at, size)] for n, at, size in left_side], 0)
+        own = joined([blocks[2 * n + c, pl.ds(at, size)] for n, c, at, size in right_side], 0)
+        logit = dot(rest, own, NT)
         value = jnp.tanh(logit * slope + shift) * 8.0
-        row = jnp.concatenate([ids[at, 0:1, :], ids[at + 1, 0:1, :]], axis=1).astype(F32)
-        col = jnp.broadcast_to(ids[OTHER0 + a, 0:1, :].astype(F32), (128, ROWS)).T
+        row = joined([ids[2 * n + c, 0:1, pl.ds(at, size)] for n, c, at, size in right_side], 1).astype(F32)
+        col = joined([cols[n, pl.ds(at, size)] for n, at, size in left_side], 0)
         same = jnp.concatenate([col] * 4, axis=1) == row
-        value = value + jnp.where(same, -8.0, 8.0)
-        pair[pl.ds(a * ROWS, ROWS), pl.ds(b * 2 * ROWS, 2 * ROWS)] = value.astype(BF16)
+        value = (value + jnp.where(same, -8.0, 8.0)).astype(BF16)
+        first = 0
+        for n, at, size in left_side:
+            begin = 0
+            for m, c, start, width in right_side:
+                pair[pl.ds(n * ROWS + at, size), pl.ds((2 * m + c) * ROWS + start, width)] = value[
+                    first : first + size, begin : begin + width
+                ]
+                begin += width
+            first += size
 
     def y_got(m):
         q = Y_ORDER[m]
@@ -297,38 +331,51 @@
     y_got(7)
     arrived("ring_id", 2, ids.at[block(0, 2)])
     core_ids(2)
-    core_got(0)
-    unit(0, 0)
-    for q in (0, 4):
-        got_onward(0, q)
-    for q in (1, 5):
+    for n in (0, 1, 3):
+        id_columns(n)
+        core_ids_got(n)
+    core_got(0, 0, 1, 2, 3)
+    unit("0", "0")
+    core_got(1, 0, 1)
+    core_got(3, 2, 3)
+    unit("0", "early")
+    for q in (0, 4, 1, 5):
         got_onward(0, q)
     core_send(2, 0, 2)
-    got_next(0, 6)
-    got_next(0, 7)
+    for q in (4, 5):
+        got_next(1, q)
+    for q in (0, 1):
+        got_prev(1, q)
+    unit("early", "0")
+    for q in (6, 7):
+        got_next(0, q)
     core_send(1, 3)
-    got_prev(0, 2)
-    got_prev(0, 3)
+    for q in (2, 3):
+        got_prev(0, q)
     core_send(3, 1)
-    core_got(2)
-    unit(0, 2)
+    unit("early", "early")
+    core_ids_got(2)
+    core_got(2, 0, 1, 2, 3)
+    unit("0", "2")
     for q in (4, 5):
         got_next(0, q)
     core_send(1, 2)
     for q in (0, 1):
         got_prev(0, q)
     core_send(3, 0)
+    unit("early", "2")
+    arrived("ring_id", 5, ids.at[block(1, 2)])
+    id_columns(2)
     for q in (0, 4, 1, 5):
         got_onward(1, q)
     for n in range(4):
         arrived("extra", n, piece(1, 2, EXTRA[n]))
-    arrived("ring_id", 5, ids.at[block(1, 2)])
-    unit(2, 0)
-    unit(2, 2)
-    core_got(1)
-    unit(2, 1)
-    core_got(3)
-    unit(2, 3)
+    unit("2", "0")
+    unit("2", "2")
+    unit("2", "early")
+    core_got(1, 2, 3)
+    core_got(3, 0, 1)
+    unit("2", "late")
 
     def own_terms(half, slot):
         rest = blocks[pl.ds(OTHER0, 4)].reshape(4 * ROWS, EMB)
@@ -421,31 +468,25 @@
     send_far(1)
     for q in (2, 6, 3, 7):
         got_next(1, q)
-    for q in (5, 4):
-        got_next(1, q)
-    for q in (0, 1, 2, 3, 6, 7):
+    for q in (2, 6, 3, 7):
         got_prev(1, q)
-    unit(3, 2)
-    unit(1, 2)
+    unit("late", "2")
     give(2)
-    unit(3, 0)
-    unit(3, 1)
-    unit(3, 3)
+    unit("late", "0")
+    unit("late", "early")
+    unit("late", "late")
+    unit("early", "late")
+    keep(2)
+    send_far(0)
     other_terms(3)
     send_extra(3)
     send_near(1, 3, (4, 5), next_copy)
-    keep(2)
-    send_far(0)
-    unit(1, 0)
-    unit(1, 1)
-    unit(1, 3)
     other_terms(1)
     send_extra(1)
     send_near(1, 1, (2, 3), prev_copy)
     send_near(1, 3, (0, 1, 2, 3), next_copy)
     send_near(1, 1, (4, 5, 6, 7), prev_copy)
-    unit(0, 1)
-    unit(0, 3)
+    unit("0", "late")
     give(3)
     give(1)
     other_terms(0)
@@ -459,8 +500,9 @@
         send_near(0, 1, (n + 4,), prev_copy)
     send_near(0, 3, (6, 7), next_copy)
     send_near(0, 1, (0, 1), prev_copy)
+    send_back(BACK_ORDER[2:4])
     give(0)
-    send_back(BACK_ORDER[2:6])
+    send_back(BACK_ORDER[4:6])
     keep(0)
     send_back(BACK_ORDER[6:])
 
@@ -503,6 +545,9 @@
         here = pl.ds(pl.multiple_of(n * 256, 256), 256)
         sg_ref[:, here] = dot(rg[...], w_ref[here, :], NT).astype(BF16)
 
+    sg_copy = pltpu.make_async_copy(sg_ref, sg_hbm, lsem.at[4 + QUARTERS])
+    sg_copy.start()
+
     def group(n, dy, d):
         y = jnp.where(dy == 0, yh, 1 - yh)
         g = y * 4 + lax.rem(px + d, 4) if n == 0 else lax.rem(pz + d, 4) * 2 + y
@@ -542,6 +587,7 @@
     pg_ref[:, 0, :HALF] = jnp.where(core == 0, mine, got)
     pg_ref[:, 0, HALF:] = jnp.where(core == 0, got, mine)
 
+    sg_copy.wait()
     some = blocks.at[0]
     for q in range(QS):
         left("y", q, some.at[rows(q)])
@@ -583,6 +629,8 @@
     scratch = [
         ((ROWS, FEAT), BF16),
         ((FEAT, EMB), BF16),
+        ((4, ROWS, 128), F32),
+        ((ROWS, FEAT), BF16),
         ((1, ROWS), jnp.int32),
         None,
         None,
@@ -623,9 +671,9 @@
             jax.ShapeDtypeStruct((20, 1, EMB), F32),
         ),
         in_specs=[hbm] * 5,
-        out_specs=(vmem, vmem),
+        out_specs=(hbm, vmem),
         scratch_shapes=[pltpu.VMEM(*what) if what else pltpu.SMEM((1,), F32) for what in scratch]
-        + [pltpu.SemaphoreType.DMA((6,))]
+        + [pltpu.SemaphoreType.DMA((5 + QUARTERS,))]
         + [pltpu.SemaphoreType.DMA((Sems.total(),)), pltpu.SemaphoreType.DMA((Sems.total(),))],
         compiler_params=pltpu.CompilerParams(
             collective_id=0, has_side_effects=True, vmem_limit_bytes=60 * 2**20

time: 87.2 us -> 87.3 us (level)
  no operation moved by 1% of the time
where the time goes in v6:
time: 87.3 us; the launch traced here: 87.1 us
  Pallas kernels  81.7 us (94%)
  local copies, waits for them, and re-layouts  3.49 us (4%)
  between operations  1.93 us (2%)
    pallas_call x1, Pallas kernels, local(): pl.pallas_call(kernel, out_shape=(jax.ShapeDtypeStruct((ROWS, FEAT), BF16...  81.7 us
    unnamed x2, local copies, waits for them, and re-layouts  3.49 us

profile of v6, /device:TPU:1, one launch (start us, length us, event | category | flops | bytes accessed | tf_op | source)
XLA Modules:
  0.0 87.1 jit_solution(7907983877442267061)
XLA Ops:
  1.9 81.7 %contrast.1 = (bf16[256,1280]{1,0:T(8,128)(2,1)}, f32[20,1,1024]{2,1,0:T(1,128)}) custom-call(bf16[256,1280]{1,0:T(8,128)(2,1)} %bitcast.7, bf16[1280,1024]{1,0:T(8,128)(2,1)} %bitcast.5, s32[1,256]{1,0:T(1,128)} %bitcast.9, f32[1]{0:T(128)S(6)} %copy.9.lt_hbm, f32[1]{0:T(128)S(6)} %copy.10.of_hbm), custom_call_target="tpu_custom_call" | custom-call | tf_op jit(solution)/shard_map/contrast/pallas_call | solution.py:667
  83.6 2.0 %copy.11 = bf16[1,256,1280]{2,1,0:T(8,128)(2,1)} copy(bf16[1,256,1280]{2,1,0:T(8,128)(2,1)} %bitcast.6) | data formatting | bytes 1310720
  85.6 1.5 %copy.12 = f32[1,20,1024]{2,0,1:T(1,128)} copy(f32[1,20,1024]{2,0,1:T(1,128)} %bitcast.8) | data formatting | bytes 163840

commit v7 on v6

--- a/solution.py
+++ b/solution.py
@@ -56,8 +56,8 @@
 
 
 def kernel(
-    s_hbm, w_hbm, id_hbm, lt_hbm, of_hbm, sg_hbm, pg_ref,
-    s_ref, w_ref, cols, sg_ref, id_ref, lt_ref, of_ref, blocks, ids, raw, inv, pair, grad, out_buf, far_in, near_in, extra_out, extra_in, part_out, part_in, y_out, y_in,
+    s_hbm, w_hbm, id_hbm, lt_hbm, of_hbm, sg_ref, pg_ref,
+    s_ref, w_ref, cols, id_ref, lt_ref, of_ref, blocks, ids, raw, inv, pair, grad, out_buf, far_in, near_in, extra_out, extra_in, part_out, part_in, y_out, y_in,
     rg, rg_mine, rg_theirs, s_other, s_t, s_x, tall, st_out, st_in, st_sum, end_out, end_in, last_out, last_in,
     lsem, ssem, rsem,
 ):
@@ -545,9 +545,6 @@
         here = pl.ds(pl.multiple_of(n * 256, 256), 256)
         sg_ref[:, here] = dot(rg[...], w_ref[here, :], NT).astype(BF16)
 
-    sg_copy = pltpu.make_async_copy(sg_ref, sg_hbm, lsem.at[4 + QUARTERS])
-    sg_copy.start()
-
     def group(n, dy, d):
         y = jnp.where(dy == 0, yh, 1 - yh)
         g = y * 4 + lax.rem(px + d, 4) if n == 0 else lax.rem(pz + d, 4) * 2 + y
@@ -587,7 +584,6 @@
     pg_ref[:, 0, :HALF] = jnp.where(core == 0, mine, got)
     pg_ref[:, 0, HALF:] = jnp.where(core == 0, got, mine)
 
-    sg_copy.wait()
     some = blocks.at[0]
     for q in range(QS):
         left("y", q, some.at[rows(q)])
@@ -630,7 +626,6 @@
         ((ROWS, FEAT), BF16),
         ((FEAT, EMB), BF16),
         ((4, ROWS, 128), F32),
-        ((ROWS, FEAT), BF16),
         ((1, ROWS), jnp.int32),
         None,
         None,
@@ -667,13 +662,13 @@
     state_grad, owned = pl.pallas_call(
         kernel,
         out_shape=(
-            jax.ShapeDtypeStruct((ROWS, FEAT), BF16),
-            jax.ShapeDtypeStruct((20, 1, EMB), F32),
+            pltpu.VMEM((ROWS, FEAT), BF16),
+            pltpu.VMEM((20, 1, EMB), F32),
         ),
         in_specs=[hbm] * 5,
-        out_specs=(hbm, vmem),
+        out_specs=(vmem, vmem),
         scratch_shapes=[pltpu.VMEM(*what) if what else pltpu.SMEM((1,), F32) for what in scratch]
-        + [pltpu.SemaphoreType.DMA((5 + QUARTERS,))]
+        + [pltpu.SemaphoreType.DMA((4 + QUARTERS,))]
         + [pltpu.SemaphoreType.DMA((Sems.total(),)), pltpu.SemaphoreType.DMA((Sems.total(),))],
         compiler_params=pltpu.CompilerParams(
             collective_id=0, has_side_effects=True, vmem_limit_bytes=60 * 2**20

time: 87.3 us -> 84.6 us (0.969)
  local copies, waits for them, and re-layouts: 3.49 us -> 1.47 us
    unnamed x2, local copies, waits for them, and re-layouts: 3.49 us -> 1.47 us
where the time goes in v7:
time: 84.6 us; the launch traced here: 84.4 us
  Pallas kernels  81 us (96%)
  between operations  1.93 us (2%)
  local copies, waits for them, and re-layouts  1.47 us (2%)
    pallas_call x1, Pallas kernels, local(): pl.pallas_call(kernel, out_shape=(pltpu.VMEM((ROWS, FEAT), BF16), pltpu.V...  81 us

profile of v7, /device:TPU:1, one launch (start us, length us, event | category | flops | bytes accessed | tf_op | source)
XLA Modules:
  0.0 84.4 jit_solution(3733480094173788480)
XLA Ops:
  1.9 81.0 %contrast.1 = (bf16[256,1280]{1,0:T(8,128)(2,1)S(1)}, f32[20,1,1024]{2,1,0:T(1,128)S(1)}) custom-call(bf16[256,1280]{1,0:T(8,128)(2,1)} %bitcast.8, bf16[1280,1024]{1,0:T(8,128)(2,1)} %bitcast.7, s32[1,256]{1,0:T(1,128)} %bitcast.9, f32[1]{0:T(128)S(6)} %copy.11.lt_hbm, f32[1]{0:T(128)S(6)} %copy.12.of_hbm), custom_call_target="tpu_custom_call" | custom-call | tf_op jit(solution)/shard_map/contrast/pallas_call | solution.py:662
  83.0 0.8 copy.9
  83.8 0.6 copy.10

commit v8 on v7

--- a/solution.py
+++ b/solution.py
@@ -21,6 +21,7 @@
 QUARTERS = 4
 FEAT_Z = FEAT // 4
 OWN_ROWS = 40
+PADDED = 48
 OTHER0 = 8
 
 Y_ORDER = (0, 4, 1, 5, 2, 6, 3, 7)
@@ -34,7 +35,7 @@
     sizes = dict(
         y=QS, y_id=1, ring=2 * 3 * QS, ring_id=2 * 3, core=16, core_id=4, core_s=1, extra=4,
         part=4, far=2 * QS, to_next=2 * QS, to_prev=2 * QS, y_extra=4, y_back=QS,
-        rg=QS, st=8, end=16, last=1,
+        rg=QS, st=16, end=32, last=1,
     )
 
     @classmethod
@@ -114,8 +115,7 @@
         return blocks.at[block(k, slot), rows(q)]
 
     barrier = pltpu.get_barrier_semaphore()
-    near = [partner, y_up, y_down, plane(0, 1, 0)]
-    near += [plane(n, dy, d) for n in range(2) for dy in range(2) for d in (1, 2, 3)]
+    near = [partner, y_up, y_down] + [plane(n, 0, d) for n in range(2) for d in (1, 3)]
     for where in near:
         pl.semaphore_signal(barrier, inc=1, device_id=where, device_id_type=MESH)
 
@@ -373,9 +373,6 @@
     unit("2", "0")
     unit("2", "2")
     unit("2", "early")
-    core_got(1, 2, 3)
-    core_got(3, 0, 1)
-    unit("2", "late")
 
     def own_terms(half, slot):
         rest = blocks[pl.ds(OTHER0, 4)].reshape(4 * ROWS, EMB)
@@ -385,11 +382,18 @@
         for n in range(2):
             cols = halves(n)
             own = blocks[pl.ds(0, 8), :, cols].reshape(8 * ROWS, HALF)
-            value = dot(pair[pl.ds(slot * ROWS, ROWS), :], own, NN)
-            if slot == 2:
-                out_buf[1, 2, :, cols] = value.astype(BF16)
+            grad[1, slot, :, cols] = dot(pair[pl.ds(slot * ROWS, ROWS), :], own, NN)
+
+    def far_terms(names, last):
+        what = [one for name in names for one in own_rows_of[name]]
+        terms = joined([pair[pl.ds(2 * ROWS, ROWS), pl.ds((2 * m + c) * ROWS + at, size)] for m, c, at, size in what], 1)
+        for n in range(2):
+            own = joined([blocks[2 * m + c, pl.ds(at, size), halves(n)] for m, c, at, size in what], 0)
+            value = dot(terms, own, NN)
+            if last:
+                out_buf[1, 2, :, halves(n)] = (grad[1, 2, :, halves(n)] + value).astype(BF16)
             else:
-                grad[1, slot, :, cols] = value
+                grad[1, 2, :, halves(n)] = value
 
     def give(slot):
         part_out[slot] = own_terms(1, slot).astype(BF16)
@@ -464,7 +468,11 @@
             y_out[rows(q), :] = reduced(1, q).astype(BF16)
             back_copy(q).start()
 
-    other_terms(2)
+    far_terms(("0", "2", "early"), False)
+    core_got(1, 2, 3)
+    core_got(3, 0, 1)
+    unit("2", "late")
+    far_terms(("late",), True)
     send_far(1)
     for q in (2, 6, 3, 7):
         got_next(1, q)
@@ -530,49 +538,60 @@
         at = pl.multiple_of(lax.rem((px if n else pz) + d, 4) * FEAT_Z, FEAT_Z)
         return dot((s_x if n else s_t)[pl.ds(at, FEAT_Z), :], rg_mine[:, pl.ds(256 * n, 256)], NN)
 
-    def st_copy(n, d):
-        return copy("st", 4 * n + d, st_out.at[n, d], st_in.at[n, d], ring_x(d) if n else ring_z(d))
+    def st_copy(n, h, d):
+        return copy("st", 8 * n + 4 * h + d, st_out.at[n, h, d], st_in.at[n, h, d], ring_x(d) if n else ring_z(d))
 
     for d in (2, 1, 3):
         for n in range(2):
-            st_out[n, d] = part_of(n, d).astype(BF16)
-            st_copy(n, d).start()
+            value = part_of(n, d).astype(BF16)
+            for h in range(2):
+                st_out[n, h, d] = value[:, 128 * h : 128 * h + 128]
+            st_copy(n, 0, d).start()
+    for d in (2, 1, 3):
+        for n in range(2):
+            st_copy(n, 1, d).start()
     for n in range(2):
-        st_sum[n] = part_of(n, 0)
+        value = part_of(n, 0)
+        for h in range(2):
+            st_sum[n, h] = value[:, 128 * h : 128 * h + 128]
 
     @pl.loop(0, FEAT // 256)
     def _(n):
         here = pl.ds(pl.multiple_of(n * 256, 256), 256)
         sg_ref[:, here] = dot(rg[...], w_ref[here, :], NT).astype(BF16)
 
-    def group(n, dy, d):
+    def group(n, h, dy, d):
         y = jnp.where(dy == 0, yh, 1 - yh)
         g = y * 4 + lax.rem(px + d, 4) if n == 0 else lax.rem(pz + d, 4) * 2 + y
-        return st_sum[n, pl.ds(pl.multiple_of(g * OWN_ROWS, 8), OWN_ROWS), :]
-
-    def stacked(value):
-        return jnp.concatenate([value[:, :128], value[:, 128:]], axis=0)
-
-    def end_copy(n, k):
-        return copy("end", 8 * n + k, end_out.at[n, k], end_in.at[n, k], plane(n, k // 4, k % 4))
-
-    for n in range(2):
-        for d in (1, 3, 2):
-            arrived("st", 4 * n + d, st_in.at[n, d])
-        st_sum[n] += st_in[n, 1].astype(F32) + st_in[n, 2].astype(F32) + st_in[n, 3].astype(F32)
-        for k in (6, 5, 7, 4, 2, 1, 3):
-            end_out[n, k] = stacked(group(n, k // 4, k % 4)).astype(BF16)
-            end_copy(n, k).start()
-
-    def finished(n):
-        total = stacked(group(n, 0, 0))
+        return st_sum[n, h, pl.ds(pl.multiple_of(g * OWN_ROWS, 8), OWN_ROWS), :]
+
+    def end_copy(n, h, k):
+        m = 16 * n + 8 * h + k
+        return copy("end", m, end_out.at[n, h, k], end_in.at[n, h, k], plane(n, k // 4, k % 4))
+
+    pad = jnp.zeros((PADDED - OWN_ROWS, 128), F32)
+    for h in range(2):
+        for n in range(2):
+            for d in (1, 3, 2):
+                arrived("st", 8 * n + 4 * h + d, st_in.at[n, h, d])
+            st_sum[n, h] += (
+                st_in[n, h, 1].astype(F32) + st_in[n, h, 2].astype(F32) + st_in[n, h, 3].astype(F32)
+            )
+            for k in (6, 5, 7, 4, 2, 1, 3):
+                value = jnp.concatenate([group(n, h, k // 4, k % 4), pad], axis=0)
+                end_out[n, h, k] = value.astype(BF16)
+                end_copy(n, h, k).start()
+
+    def finished(n, h):
+        total = group(n, h, 0, 0)
         for k in (1, 3, 2, 4, 5, 7, 6):
-            arrived("end", 8 * n + k, end_in.at[n, k])
-            total += end_in[n, k].astype(F32)
-        return jnp.concatenate([total[:OWN_ROWS], total[OWN_ROWS:]], axis=1)
-
-    p_fin = finished(0)
-    q_fin = finished(1)
+            arrived("end", 16 * n + 8 * h + k, end_in.at[n, h, k])
+            total += end_in[n, h, k].astype(F32)[:OWN_ROWS]
+        return total
+
+    quarters = {(n, h): finished(n, h) for h in range(2) for n in range(2)}
+    p_fin = jnp.concatenate([quarters[0, 0], quarters[0, 1]], axis=1)
+    q_fin = jnp.concatenate([quarters[1, 0], quarters[1, 1]], axis=1)
     both = jnp.concatenate([p_fin, q_fin], axis=1)
     first, second = both[:20], both[20:]
     theirs = jnp.where(core == 0, second, first)
@@ -612,10 +631,11 @@
         left("y_extra", n, some.at[rows(0)])
     left("core_s", 0, s_other)
     for n in range(2):
-        for d in (1, 2, 3):
-            left("st", 4 * n + d, st_out.at[n, d])
-        for k in range(1, 8):
-            left("end", 8 * n + k, end_out.at[n, k])
+        for h in range(2):
+            for d in (1, 2, 3):
+                left("st", 8 * n + 4 * h + d, st_out.at[n, h, d])
+            for k in range(1, 8):
+                left("end", 16 * n + 8 * h + k, end_out.at[n, h, k])
     left("last", 0, last_out)
 
 
@@ -651,11 +671,11 @@
         ((FEAT, 2 * ROWS), BF16),
         ((FEAT, 2 * ROWS), BF16),
         ((FEAT, ROWS), F32),
-        ((2, 4, FEAT_Z, 256), BF16),
-        ((2, 4, FEAT_Z, 256), BF16),
-        ((2, FEAT_Z, 256), F32),
-        ((2, 8, 2 * OWN_ROWS, 128), BF16),
-        ((2, 8, 2 * OWN_ROWS, 128), BF16),
+        ((2, 2, 4, FEAT_Z, 128), BF16),
+        ((2, 2, 4, FEAT_Z, 128), BF16),
+        ((2, 2, FEAT_Z, 128), F32),
+        ((2, 2, 8, PADDED, 128), BF16),
+        ((2, 2, 8, PADDED, 128), BF16),
         ((24, HALF), F32),
         ((24, HALF), F32),
     ]

time: 84.6 us -> 84 us (level)
  no operation moved by 1% of the time
where the time goes in v8:
time: 84 us; the launch traced here: 83.9 us
  Pallas kernels  80.5 us (96%)
  between operations  1.93 us (2%)
  local copies, waits for them, and re-layouts  1.47 us (2%)
    pallas_call x1, Pallas kernels, local(): pl.pallas_call(kernel, out_shape=(pltpu.VMEM((ROWS, FEAT), BF16), pltpu.V...  80.5 us

profile of v8, /device:TPU:1, one launch (start us, length us, event | category | flops | bytes accessed | tf_op | source)
XLA Modules:
  0.0 83.9 jit_solution(17890139188765510793)
XLA Ops:
  1.9 80.5 %contrast.1 = (bf16[256,1280]{1,0:T(8,128)(2,1)S(1)}, f32[20,1,1024]{2,1,0:T(1,128)S(1)}) custom-call(bf16[256,1280]{1,0:T(8,128)(2,1)} %bitcast.8, bf16[1280,1024]{1,0:T(8,128)(2,1)} %bitcast.7, s32[1,256]{1,0:T(1,128)} %bitcast.9, f32[1]{0:T(128)S(6)} %copy.11.lt_hbm, f32[1]{0:T(128)S(6)} %copy.12.of_hbm), custom_call_target="tpu_custom_call" | custom-call | tf_op jit(solution)/shard_map/contrast/pallas_call | solution.py:682
  82.4 0.8 copy.9
  83.3 0.6 copy.10

commit v9 on v8

--- a/solution.py
+++ b/solution.py
@@ -28,7 +28,6 @@
 NEXT_ORDER = (2, 3, 0, 1, 6, 7, 4, 5)
 PREV_ORDER = (6, 7, 4, 5, 2, 3, 0, 1)
 EXTRA = (2, 6, 3, 7)
-BACK_ORDER = (4, 5, 6, 0, 7, 1, 2, 3)
 
 
 class Sems:
@@ -294,86 +293,6 @@
         got_onward(0, EXTRA[n])
         extra(n).start()
 
-    y_got(0)
-    own_on(0)
-    y_got(1)
-    own_on(1)
-    ids_onward(0)
-    core_ids(1)
-    core_ids(3)
-    arrived("y_id", 0, ids.at[OTHER0])
-    ids_out(1)
-    arrived("core_s", 0, s_other)
-    turn(s_other, ROWS)
-    y_got(2)
-    own_on(2)
-    y_got(3)
-    own_on(3)
-    for q in (7, 4, 5):
-        to_next(0, q).start()
-    for q in (3, 0, 1):
-        to_prev(0, q).start()
-    core_send(1, 0, 1)
-    core_send(3, 2, 3)
-    other_on(0)
-    y_got(4)
-    other_on(4)
-    y_got(5)
-    far_on(0)
-    far_on(1)
-    ids_onward(1)
-    other_on(1)
-    y_got(6)
-    far_on(2)
-    far_on(3)
-    core_send(2, 1, 3)
-    other_on(5)
-    y_got(7)
-    arrived("ring_id", 2, ids.at[block(0, 2)])
-    core_ids(2)
-    for n in (0, 1, 3):
-        id_columns(n)
-        core_ids_got(n)
-    core_got(0, 0, 1, 2, 3)
-    unit("0", "0")
-    core_got(1, 0, 1)
-    core_got(3, 2, 3)
-    unit("0", "early")
-    for q in (0, 4, 1, 5):
-        got_onward(0, q)
-    core_send(2, 0, 2)
-    for q in (4, 5):
-        got_next(1, q)
-    for q in (0, 1):
-        got_prev(1, q)
-    unit("early", "0")
-    for q in (6, 7):
-        got_next(0, q)
-    core_send(1, 3)
-    for q in (2, 3):
-        got_prev(0, q)
-    core_send(3, 1)
-    unit("early", "early")
-    core_ids_got(2)
-    core_got(2, 0, 1, 2, 3)
-    unit("0", "2")
-    for q in (4, 5):
-        got_next(0, q)
-    core_send(1, 2)
-    for q in (0, 1):
-        got_prev(0, q)
-    core_send(3, 0)
-    unit("early", "2")
-    arrived("ring_id", 5, ids.at[block(1, 2)])
-    id_columns(2)
-    for q in (0, 4, 1, 5):
-        got_onward(1, q)
-    for n in range(4):
-        arrived("extra", n, piece(1, 2, EXTRA[n]))
-    unit("2", "0")
-    unit("2", "2")
-    unit("2", "early")
-
     def own_terms(half, slot):
         rest = blocks[pl.ds(OTHER0, 4)].reshape(4 * ROWS, EMB)
         return dot(pair[:, pl.ds((2 * slot + half) * ROWS, ROWS)], rest, TN)
@@ -468,56 +387,10 @@
             y_out[rows(q), :] = reduced(1, q).astype(BF16)
             back_copy(q).start()
 
-    far_terms(("0", "2", "early"), False)
-    core_got(1, 2, 3)
-    core_got(3, 0, 1)
-    unit("2", "late")
-    far_terms(("late",), True)
-    send_far(1)
-    for q in (2, 6, 3, 7):
-        got_next(1, q)
-    for q in (2, 6, 3, 7):
-        got_prev(1, q)
-    unit("late", "2")
-    give(2)
-    unit("late", "0")
-    unit("late", "early")
-    unit("late", "late")
-    unit("early", "late")
-    keep(2)
-    send_far(0)
-    other_terms(3)
-    send_extra(3)
-    send_near(1, 3, (4, 5), next_copy)
-    other_terms(1)
-    send_extra(1)
-    send_near(1, 1, (2, 3), prev_copy)
-    send_near(1, 3, (0, 1, 2, 3), next_copy)
-    send_near(1, 1, (4, 5, 6, 7), prev_copy)
-    unit("0", "late")
-    give(3)
-    give(1)
-    other_terms(0)
-    keep(3)
-    send_near(0, 3, (4, 5), next_copy)
-    keep(1)
-    send_near(0, 1, (2, 3), prev_copy)
-    send_back(BACK_ORDER[:2])
-    for n in range(4):
-        send_near(0, 3, (n,), next_copy)
-        send_near(0, 1, (n + 4,), prev_copy)
-    send_near(0, 3, (6, 7), next_copy)
-    send_near(0, 1, (0, 1), prev_copy)
-    send_back(BACK_ORDER[2:4])
-    give(0)
-    send_back(BACK_ORDER[4:6])
-    keep(0)
-    send_back(BACK_ORDER[6:])
-
     def rg_copy(q):
         return copy("rg", q, rg_theirs.at[rows(q)], rg_mine.at[pl.ds(ROWS + CHUNK * q, CHUNK)], partner)
 
-    for q in BACK_ORDER:
+    def finish(q):
         total = reduced(0, q)
         arrived("y_back", q, y_in.at[rows(q)])
         emb_grad = temper * (total + y_in[rows(q), :].astype(F32))
@@ -530,6 +403,175 @@
         rg_mine[rows(q), :] = jnp.where(core == 0, low, high)
         rg_theirs[rows(q), :] = jnp.where(core == 0, high, low)
         rg_copy(q).start()
+
+    arrived("y_id", 0, ids.at[OTHER0])
+    ids_out(1)
+    y_got(0)
+    y_got(1)
+    y_got(2)
+    ids_onward(1)
+    own_on(0)
+    ids_onward(0)
+    own_on(3)
+    y_got(3)
+    y_got(4)
+    own_on(1)
+    y_got(5)
+    own_on(2)
+    core_send(1, 0, 1)
+    core_send(3, 2, 3)
+    y_got(6)
+    to_next(0, 5).start()
+    to_prev(0, 1).start()
+    to_next(0, 4).start()
+    far_on(0)
+    far_on(3)
+    got_onward(0, 5)
+    far_on(1)
+    y_got(7)
+    core_ids(1)
+    core_ids(3)
+    core_got(0, 0, 1, 2, 3)
+    to_next(0, 7).start()
+    got_onward(0, 1)
+    core_got(3, 2, 3)
+    got_next(1, 4)
+    got_next(1, 5)
+    got_prev(1, 0)
+    got_prev(1, 1)
+    other_on(5)
+    to_prev(0, 0).start()
+    other_on(4)
+    other_on(1)
+    arrived("core_s", 0, s_other)
+    turn(s_other, ROWS)
+    id_columns(1)
+    id_columns(3)
+    core_ids_got(1)
+    core_ids_got(3)
+    core_got(1, 0, 1)
+    got_onward(0, 0)
+    id_columns(0)
+    core_ids_got(0)
+    far_on(2)
+    other_on(0)
+    got_onward(0, 4)
+    unit("0", "early")
+    arrived("ring_id", 2, ids.at[block(0, 2)])
+    core_ids(2)
+    core_send(2, 1, 3)
+    core_send(2, 0, 2)
+    to_prev(0, 3).start()
+    unit("early", "early")
+    unit("0", "0")
+    unit("early", "0")
+    core_ids_got(2)
+    core_got(2, 0, 1, 2, 3)
+    got_next(1, 2)
+    got_prev(1, 2)
+    got_next(1, 6)
+    got_prev(1, 6)
+    got_next(1, 3)
+    got_prev(1, 3)
+    got_next(1, 7)
+    got_prev(1, 7)
+    got_prev(0, 0)
+    got_prev(0, 1)
+    core_send(3, 0)
+    unit("late", "2")
+    unit("late", "early")
+    unit("late", "0")
+    unit("0", "2")
+    got_prev(0, 2)
+    got_prev(0, 3)
+    core_send(3, 1)
+    got_next(0, 4)
+    got_next(0, 5)
+    core_send(1, 2)
+    unit("early", "2")
+    arrived("ring_id", 5, ids.at[block(1, 2)])
+    id_columns(2)
+    got_next(0, 6)
+    got_next(0, 7)
+    core_send(1, 3)
+    arrived("extra", 0, piece(1, 2, EXTRA[0]))
+    arrived("extra", 1, piece(1, 2, EXTRA[1]))
+    arrived("extra", 2, piece(1, 2, EXTRA[2]))
+    arrived("extra", 3, piece(1, 2, EXTRA[3]))
+    got_onward(1, 0)
+    got_onward(1, 4)
+    got_onward(1, 1)
+    got_onward(1, 5)
+    unit("2", "2")
+    unit("2", "early")
+    unit("2", "0")
+    far_terms(("0", "2", "early"), False)
+    core_got(1, 2, 3)
+    core_got(3, 0, 1)
+    unit("2", "late")
+    far_terms(("late",), True)
+    send_far(1)
+    give(2)
+    unit("early", "late")
+    unit("late", "late")
+    other_terms(3)
+    send_extra(3)
+    keep(2)
+    send_far(0)
+    unit("0", "late")
+    give(1)
+    give(3)
+    send_near(1, 3, (1,), next_copy)
+    other_terms(1)
+    send_extra(1)
+    send_near(1, 3, (0,), next_copy)
+    send_near(1, 1, (6,), prev_copy)
+    other_terms(0)
+    send_near(1, 1, (7,), prev_copy)
+    keep(1)
+    keep(3)
+    send_near(0, 1, (2,), prev_copy)
+    send_near(0, 3, (4,), next_copy)
+    send_back((1,))
+    send_near(1, 3, (2,), next_copy)
+    send_near(1, 1, (2,), prev_copy)
+    send_near(1, 3, (5,), next_copy)
+    send_near(0, 1, (4,), prev_copy)
+    send_near(1, 1, (5,), prev_copy)
+    send_near(0, 3, (0,), next_copy)
+    send_near(0, 1, (5,), prev_copy)
+    send_back((6,))
+    send_near(1, 3, (4,), next_copy)
+    send_near(0, 1, (0,), prev_copy)
+    send_near(0, 3, (2,), next_copy)
+    give(0)
+    send_near(0, 3, (5,), next_copy)
+    send_near(0, 3, (1,), next_copy)
+    send_near(0, 1, (1,), prev_copy)
+    send_near(1, 1, (4,), prev_copy)
+    send_near(1, 3, (3,), next_copy)
+    send_near(0, 3, (7,), next_copy)
+    send_back((0,))
+    send_back((7,))
+    keep(0)
+    send_near(0, 3, (6,), next_copy)
+    send_back((2,))
+    send_near(0, 3, (3,), next_copy)
+    send_near(1, 1, (3,), prev_copy)
+    send_near(0, 1, (6,), prev_copy)
+    send_near(0, 1, (7,), prev_copy)
+    send_near(0, 1, (3,), prev_copy)
+    send_back((5,))
+    send_back((4,))
+    send_back((3,))
+    finish(1)
+    finish(2)
+    finish(6)
+    finish(0)
+    finish(4)
+    finish(7)
+    finish(5)
+    finish(3)
 
     for q in range(QS):
         arrived("rg", q, rg_mine.at[pl.ds(ROWS + CHUNK * q, CHUNK)])

time: 84 us -> 82.8 us (0.986)
  Pallas kernels: 80.5 us -> 79.3 us
    pallas_call x1, Pallas kernels: 80.5 us -> 79.3 us  [local(): pl.pallas_call(kernel, out_shape=(pltpu.VMEM((ROWS, FEAT), BF16), pltpu.V...]
where the time goes in v9:
time: 82.8 us; the launch traced here: 82.7 us
  Pallas kernels  79.3 us (96%)
  between operations  1.93 us (2%)
  local copies, waits for them, and re-layouts  1.47 us (2%)
    pallas_call x1, Pallas kernels, local(): pl.pallas_call(kernel, out_shape=(pltpu.VMEM((ROWS, FEAT), BF16), pltpu.V...  79.3 us

profile of v9, /device:TPU:1, one launch (start us, length us, event | category | flops | bytes accessed | tf_op | source)
XLA Modules:
  0.0 82.7 jit_solution(1301551395954258423)
XLA Ops:
  1.9 79.3 %contrast.1 = (bf16[256,1280]{1,0:T(8,128)(2,1)S(1)}, f32[20,1,1024]{2,1,0:T(1,128)S(1)}) custom-call(bf16[256,1280]{1,0:T(8,128)(2,1)} %bitcast.8, bf16[1280,1024]{1,0:T(8,128)(2,1)} %bitcast.7, s32[1,256]{1,0:T(1,128)} %bitcast.9, f32[1]{0:T(128)S(6)} %copy.11.lt_hbm, f32[1]{0:T(128)S(6)} %copy.12.of_hbm), custom_call_target="tpu_custom_call" | custom-call | tf_op jit(solution)/shard_map/contrast/pallas_call | solution.py:724
  81.2 0.8 %copy.9 = bf16[1,256,1280]{2,1,0:T(8,128)(2,1)} copy(bf16[1,256,1280]{2,1,0:T(8,128)(2,1)S(1)} %bitcast.5) | data formatting | bytes 1310720
  82.1 0.6 copy.10

commit v10 on v9

--- a/solution.py
+++ b/solution.py
@@ -408,63 +408,71 @@
     ids_out(1)
     y_got(0)
     y_got(1)
+    ids_onward(1)
+    core_got(0, 0, 1, 2, 3)
+    own_on(1)
+    ids_onward(0)
+    own_on(0)
+    own_on(2)
     y_got(2)
-    ids_onward(1)
-    own_on(0)
-    ids_onward(0)
     own_on(3)
-    y_got(3)
-    y_got(4)
-    own_on(1)
-    y_got(5)
-    own_on(2)
-    core_send(1, 0, 1)
-    core_send(3, 2, 3)
-    y_got(6)
-    to_next(0, 5).start()
-    to_prev(0, 1).start()
-    to_next(0, 4).start()
-    far_on(0)
-    far_on(3)
-    got_onward(0, 5)
-    far_on(1)
-    y_got(7)
     core_ids(1)
     core_ids(3)
-    core_got(0, 0, 1, 2, 3)
+    y_got(3)
+    core_send(3, 2, 3)
+    y_got(4)
+    y_got(5)
     to_next(0, 7).start()
-    got_onward(0, 1)
-    core_got(3, 2, 3)
+    far_on(1)
+    to_prev(0, 3).start()
     got_next(1, 4)
     got_next(1, 5)
     got_prev(1, 0)
     got_prev(1, 1)
+    y_got(6)
+    y_got(7)
     other_on(5)
-    to_prev(0, 0).start()
-    other_on(4)
-    other_on(1)
-    arrived("core_s", 0, s_other)
-    turn(s_other, ROWS)
+    other_on(0)
+    arrived("ring_id", 2, ids.at[block(0, 2)])
+    core_ids(2)
+    id_columns(0)
+    core_ids_got(0)
+    far_on(3)
+    to_next(0, 4).start()
+    far_on(2)
     id_columns(1)
     id_columns(3)
     core_ids_got(1)
     core_ids_got(3)
+    far_on(0)
+    core_got(3, 2, 3)
+    to_next(0, 5).start()
+    other_on(1)
+    arrived("core_s", 0, s_other)
+    turn(s_other, ROWS)
+    got_onward(0, 0)
+    other_on(4)
+    core_send(1, 0, 1)
+    to_prev(0, 1).start()
+    unit("0", "0")
+    core_send(2, 1, 3)
+    got_onward(0, 1)
+    got_onward(0, 4)
+    got_onward(0, 5)
+    to_prev(0, 0).start()
+    core_send(2, 0, 2)
     core_got(1, 0, 1)
-    got_onward(0, 0)
-    id_columns(0)
-    core_ids_got(0)
-    far_on(2)
-    other_on(0)
-    got_onward(0, 4)
+    unit("early", "early")
+    got_next(0, 6)
+    got_next(0, 7)
+    core_send(1, 3)
     unit("0", "early")
-    arrived("ring_id", 2, ids.at[block(0, 2)])
-    core_ids(2)
-    core_send(2, 1, 3)
-    core_send(2, 0, 2)
-    to_prev(0, 3).start()
-    unit("early", "early")
-    unit("0", "0")
     unit("early", "0")
+    got_prev(0, 2)
+    got_prev(0, 3)
+    core_send(3, 1)
+    arrived("ring_id", 5, ids.at[block(1, 2)])
+    id_columns(2)
     core_ids_got(2)
     core_got(2, 0, 1, 2, 3)
     got_next(1, 2)
@@ -475,102 +483,94 @@
     got_prev(1, 3)
     got_next(1, 7)
     got_prev(1, 7)
-    got_prev(0, 0)
-    got_prev(0, 1)
-    core_send(3, 0)
+    unit("early", "2")
+    unit("late", "early")
     unit("late", "2")
-    unit("late", "early")
+    unit("0", "2")
     unit("late", "0")
-    unit("0", "2")
-    got_prev(0, 2)
-    got_prev(0, 3)
-    core_send(3, 1)
-    got_next(0, 4)
-    got_next(0, 5)
-    core_send(1, 2)
-    unit("early", "2")
-    arrived("ring_id", 5, ids.at[block(1, 2)])
-    id_columns(2)
-    got_next(0, 6)
-    got_next(0, 7)
-    core_send(1, 3)
     arrived("extra", 0, piece(1, 2, EXTRA[0]))
     arrived("extra", 1, piece(1, 2, EXTRA[1]))
     arrived("extra", 2, piece(1, 2, EXTRA[2]))
     arrived("extra", 3, piece(1, 2, EXTRA[3]))
+    got_prev(0, 0)
+    got_prev(0, 1)
+    core_send(3, 0)
+    got_next(0, 4)
+    got_next(0, 5)
+    core_send(1, 2)
     got_onward(1, 0)
     got_onward(1, 4)
     got_onward(1, 1)
     got_onward(1, 5)
-    unit("2", "2")
     unit("2", "early")
     unit("2", "0")
+    unit("2", "2")
     far_terms(("0", "2", "early"), False)
+    give(2)
     core_got(1, 2, 3)
     core_got(3, 0, 1)
     unit("2", "late")
     far_terms(("late",), True)
     send_far(1)
-    give(2)
+    unit("0", "late")
     unit("early", "late")
     unit("late", "late")
     other_terms(3)
     send_extra(3)
     keep(2)
     send_far(0)
-    unit("0", "late")
+    give(3)
+    send_near(1, 3, (0,), next_copy)
     give(1)
-    give(3)
-    send_near(1, 3, (1,), next_copy)
     other_terms(1)
     send_extra(1)
-    send_near(1, 3, (0,), next_copy)
+    send_near(1, 3, (1,), next_copy)
     send_near(1, 1, (6,), prev_copy)
+    keep(3)
     other_terms(0)
+    send_near(0, 3, (4,), next_copy)
+    keep(1)
+    send_near(0, 1, (4,), prev_copy)
+    send_back((0,))
+    send_near(1, 3, (4,), next_copy)
     send_near(1, 1, (7,), prev_copy)
-    keep(1)
-    keep(3)
+    send_near(1, 1, (5,), prev_copy)
+    send_near(0, 3, (5,), next_copy)
+    send_near(1, 1, (4,), prev_copy)
     send_near(0, 1, (2,), prev_copy)
-    send_near(0, 3, (4,), next_copy)
+    send_near(1, 1, (2,), prev_copy)
     send_back((1,))
+    send_near(0, 1, (6,), prev_copy)
+    send_near(1, 3, (5,), next_copy)
+    send_near(0, 3, (2,), next_copy)
+    send_near(1, 3, (3,), next_copy)
+    give(0)
+    send_near(0, 3, (6,), next_copy)
+    send_near(0, 3, (7,), next_copy)
     send_near(1, 3, (2,), next_copy)
-    send_near(1, 1, (2,), prev_copy)
-    send_near(1, 3, (5,), next_copy)
-    send_near(0, 1, (4,), prev_copy)
-    send_near(1, 1, (5,), prev_copy)
-    send_near(0, 3, (0,), next_copy)
-    send_near(0, 1, (5,), prev_copy)
+    send_near(0, 1, (7,), prev_copy)
+    send_near(0, 1, (0,), prev_copy)
+    send_near(1, 1, (3,), prev_copy)
     send_back((6,))
-    send_near(1, 3, (4,), next_copy)
-    send_near(0, 1, (0,), prev_copy)
-    send_near(0, 3, (2,), next_copy)
-    give(0)
-    send_near(0, 3, (5,), next_copy)
+    send_back((7,))
     send_near(0, 3, (1,), next_copy)
     send_near(0, 1, (1,), prev_copy)
-    send_near(1, 1, (4,), prev_copy)
-    send_near(1, 3, (3,), next_copy)
-    send_near(0, 3, (7,), next_copy)
-    send_back((0,))
-    send_back((7,))
+    send_back((5,))
+    send_near(0, 1, (5,), prev_copy)
+    send_near(0, 3, (0,), next_copy)
+    send_near(0, 1, (3,), prev_copy)
+    send_back((4,))
+    send_near(0, 3, (3,), next_copy)
+    send_back((2,))
     keep(0)
-    send_near(0, 3, (6,), next_copy)
-    send_back((2,))
-    send_near(0, 3, (3,), next_copy)
-    send_near(1, 1, (3,), prev_copy)
-    send_near(0, 1, (6,), prev_copy)
-    send_near(0, 1, (7,), prev_copy)
-    send_near(0, 1, (3,), prev_copy)
-    send_back((5,))
-    send_back((4,))
     send_back((3,))
-    finish(1)
-    finish(2)
     finish(6)
     finish(0)
+    finish(5)
+    finish(2)
+    finish(1)
     finish(4)
     finish(7)
-    finish(5)
     finish(3)
 
     for q in range(QS):

time: 82.8 us -> 81 us (0.978)
  Pallas kernels: 79.3 us -> 77.5 us
    pallas_call x1, Pallas kernels: 79.3 us -> 77.5 us  [local(): pl.pallas_call(kernel, out_shape=(pltpu.VMEM((ROWS, FEAT), BF16), pltpu.V...]
where the time goes in v10:
time: 81 us; the launch traced here: 80.9 us
  Pallas kernels  77.5 us (96%)
  between operations  1.93 us (2%)
  local copies, waits for them, and re-layouts  1.47 us (2%)
    pallas_call x1, Pallas kernels, local(): pl.pallas_call(kernel, out_shape=(pltpu.VMEM((ROWS, FEAT), BF16), pltpu.V...  77.5 us

profile of v10, /device:TPU:1, one launch (start us, length us, event | category | flops | bytes accessed | tf_op | source)
XLA Modules:
  0.0 80.9 jit_solution(3672608468264471760)
XLA Ops:
  1.9 77.5 %contrast.1 = (bf16[256,1280]{1,0:T(8,128)(2,1)S(1)}, f32[20,1,1024]{2,1,0:T(1,128)S(1)}) custom-call(bf16[256,1280]{1,0:T(8,128)(2,1)} %bitcast.8, bf16[1280,1024]{1,0:T(8,128)(2,1)} %bitcast.7, s32[1,256]{1,0:T(1,128)} %bitcast.9, f32[1]{0:T(128)S(6)} %copy.11.lt_hbm, f32[1]{0:T(128)S(6)} %copy.12.of_hbm), custom_call_target="tpu_custom_call" | custom-call | tf_op jit(solution)/shard_map/contrast/pallas_call | solution.py:724
  79.4 0.8 %copy.9 = bf16[1,256,1280]{2,1,0:T(8,128)(2,1)} copy(bf16[1,256,1280]{2,1,0:T(8,128)(2,1)S(1)} %bitcast.5) | data formatting | bytes 1310720
  80.3 0.6 copy.10

commit v11 on v10

--- a/solution.py
+++ b/solution.py
@@ -410,33 +410,45 @@
     y_got(1)
     ids_onward(1)
     core_got(0, 0, 1, 2, 3)
-    own_on(1)
+    got_next(0, 3)
+    onward(0, 3).start()
+    got_prev(0, 7)
+    onward(0, 7).start()
     ids_onward(0)
-    own_on(0)
-    own_on(2)
+    got_next(0, 2)
+    onward(0, 2).start()
+    got_prev(0, 6)
+    onward(0, 6).start()
+    got_next(0, 0)
+    onward(0, 0).start()
+    got_prev(0, 4)
+    onward(0, 4).start()
     y_got(2)
-    own_on(3)
+    got_next(0, 1)
+    onward(0, 1).start()
+    got_prev(0, 5)
+    onward(0, 5).start()
     core_ids(1)
     core_ids(3)
+    to_next(0, 7).start()
     y_got(3)
     core_send(3, 2, 3)
     y_got(4)
     y_got(5)
-    to_next(0, 7).start()
     far_on(1)
     to_prev(0, 3).start()
     got_next(1, 4)
     got_next(1, 5)
     got_prev(1, 0)
     got_prev(1, 1)
+    arrived("ring_id", 2, ids.at[block(0, 2)])
+    core_ids(2)
+    id_columns(0)
+    core_ids_got(0)
     y_got(6)
     y_got(7)
     other_on(5)
     other_on(0)
-    arrived("ring_id", 2, ids.at[block(0, 2)])
-    core_ids(2)
-    id_columns(0)
-    core_ids_got(0)
     far_on(3)
     to_next(0, 4).start()
     far_on(2)
@@ -555,14 +567,14 @@
     send_back((7,))
     send_near(0, 3, (1,), next_copy)
     send_near(0, 1, (1,), prev_copy)
+    send_near(0, 3, (0,), next_copy)
     send_back((5,))
     send_near(0, 1, (5,), prev_copy)
-    send_near(0, 3, (0,), next_copy)
+    keep(0)
     send_near(0, 1, (3,), prev_copy)
     send_back((4,))
     send_near(0, 3, (3,), next_copy)
     send_back((2,))
-    keep(0)
     send_back((3,))
     finish(6)
     finish(0)
@@ -583,11 +595,12 @@
     def st_copy(n, h, d):
         return copy("st", 8 * n + 4 * h + d, st_out.at[n, h, d], st_in.at[n, h, d], ring_x(d) if n else ring_z(d))
 
-    for d in (2, 1, 3):
-        for n in range(2):
-            value = part_of(n, d).astype(BF16)
+    for some in ((2,), (1, 3)):
+        values = {(n, d): part_of(n, d).astype(BF16) for d in some for n in range(2)}
+        for (n, d), value in values.items():
             for h in range(2):
                 st_out[n, h, d] = value[:, 128 * h : 128 * h + 128]
+        for n, d in values:
             st_copy(n, 0, d).start()
     for d in (2, 1, 3):
         for n in range(2):
@@ -596,10 +609,8 @@
         value = part_of(n, 0)
         for h in range(2):
             st_sum[n, h] = value[:, 128 * h : 128 * h + 128]
-
-    @pl.loop(0, FEAT // 256)
-    def _(n):
-        here = pl.ds(pl.multiple_of(n * 256, 256), 256)
+    for n in range(FEAT // 256):
+        here = pl.ds(n * 256, 256)
         sg_ref[:, here] = dot(rg[...], w_ref[here, :], NT).astype(BF16)
 
     def group(n, h, dy, d):

time: 81 us -> 81 us (level)
  no operation moved by 1% of the time
where the time goes in v11:
time: 81 us; the launch traced here: 80.9 us
  Pallas kernels  77.5 us (96%)
  between operations  1.93 us (2%)
  local copies, waits for them, and re-layouts  1.47 us (2%)
    pallas_call x1, Pallas kernels, local(): pl.pallas_call(kernel, out_shape=(pltpu.VMEM((ROWS, FEAT), BF16), pltpu.V...  77.5 us

profile of v11, /device:TPU:1, one launch (start us, length us, event | category | flops | bytes accessed | tf_op | source)
XLA Modules:
  0.0 80.9 jit_solution(15881437793859602471)
XLA Ops:
  1.9 77.5 %contrast.1 = (bf16[256,1280]{1,0:T(8,128)(2,1)S(1)}, f32[20,1,1024]{2,1,0:T(1,128)S(1)}) custom-call(bf16[256,1280]{1,0:T(8,128)(2,1)} %bitcast.8, bf16[1280,1024]{1,0:T(8,128)(2,1)} %bitcast.7, s32[1,256]{1,0:T(1,128)} %bitcast.9, f32[1]{0:T(128)S(6)} %copy.11.lt_hbm, f32[1]{0:T(128)S(6)} %copy.12.of_hbm), custom_call_target="tpu_custom_call" | custom-call | tf_op jit(solution)/shard_map/contrast/pallas_call | solution.py:735
  79.4 0.8 %copy.9 = bf16[1,256,1280]{2,1,0:T(8,128)(2,1)} copy(bf16[1,256,1280]{2,1,0:T(8,128)(2,1)S(1)} %bitcast.5) | data formatting | bytes 1310720
  80.2 0.6 copy.10
